TPU v7x, 32 devices: a whole 2x2x4 slice. The times are simulated.
32 devices in a mesh: lon: 2 (over core), lat: 16 (over z, y, x).
Axes of the slice: x: 2, y: 2, z: 4, core: 2. Of those that a mesh axis runs over, the one named last changes fastest.
Arguments:
- ocean_state: bfloat16 [1, 96, 128, 256], P(None, 'lat', 'lon'), may hold values from -6 to 6
- land_sea: int32 [1, 96, 128], P(None, 'lat', 'lon'), may hold values 0 or 1
- cotangent: bfloat16 [1, 96, 128, 256], P(None, 'lat', 'lon'), may hold values from -6 to 6
- dw_kernel: float32 [7, 7, 256], replicated, may hold values from -0.875 to 0.875
- dw_bias: float32 [256], replicated, may hold values from -3 to 3
- ln_gain: float32 [256], replicated, may hold values from 0.1 to 1.9
- ln_bias: float32 [256], replicated, may hold values from -2 to 2
- w_in: bfloat16 [256, 1024], replicated, may hold values from -0.375 to 0.375
- b_in: float32 [1024], replicated, may hold values from -2 to 2
- w_out: bfloat16 [1024, 256], replicated, may hold values from -0.1875 to 0.1875
- b_out: float32 [256], replicated, may hold values from -2 to 2
- layer_scale: float32 [256], replicated, may hold values from 0.3 to 1.5
Outputs:
- output: bfloat16 [1, 96, 128, 256], P(None, 'lat', 'lon')
- grad_state: bfloat16 [1, 96, 128, 256], P(None, 'lat', 'lon')
- grad_kernel: float32 [7, 7, 256], replicated
- grad_dw_bias: float32 [256], replicated
- grad_ln_gain: float32 [256], replicated
- grad_ln_bias: float32 [256], replicated
- grad_w_in: float32 [256, 1024], replicated
- grad_b_in: float32 [1024], replicated
- grad_w_out: float32 [1024, 256], replicated
- grad_b_out: float32 [256], replicated
- grad_scale: float32 [256], replicated
All inputs are finite; a program needn't handle non-finite values. No bound on the sum of `land_sea` on one device may be relied on, other than what follows from the above.
Results may differ from a plain program's by a relative error of at most 0.0085.
Values may be sent and summed in bfloat16 or wider, within the bound.
A program may use at most 64 MiB of HBM per device.

v0:
```python
import jax
import jax.numpy as jnp
from jax import lax
from jax.sharding import PartitionSpec as P


def extended(array, sides, width, wrap):
    for axis, dim in sides:
        size, length = (lax.axis_size(axis), array.shape[dim])
        up = [(i, (i + 1) % size) for i in range(size if wrap else size - 1)]
        down = [(j, i) for i, j in up]
        last = lax.slice_in_dim(array, length - width, length, axis=dim)
        leading = lax.slice_in_dim(array, 0, width, axis=dim)
        before = lax.ppermute(last, axis, up)
        after = lax.ppermute(leading, axis, down)
        array = jnp.concatenate([before, array, after], axis=dim)
    return array


def depthwise(padded, kernel, num_rows, num_cols):
    summed = jnp.zeros((padded.shape[0], num_rows, num_cols, padded.shape[3]), jnp.float32)
    for row_off in range(7):
        for col_off in range(7):
            summed = (
                summed
                + padded[:, row_off : row_off + num_rows, col_off : col_off + num_cols, :].astype(
                    jnp.float32
                )
                * kernel[row_off, col_off]
            )
    return summed


def transposed(padded, kernel, num_rows, num_cols):
    summed = jnp.zeros((padded.shape[0], num_rows, num_cols, padded.shape[3]), jnp.float32)
    for row_off in range(7):
        for col_off in range(7):
            summed = (
                summed
                + padded[
                    :, 6 - row_off : 6 - row_off + num_rows, 6 - col_off : 6 - col_off + num_cols, :
                ].astype(jnp.float32)
                * kernel[row_off, col_off]
            )
    return summed


def kernel_terms(padded, grad_depth, num_rows, num_cols):
    grad_float = grad_depth.astype(jnp.float32)
    rows_out = []
    for row_off in range(7):
        cols_out = []
        for col_off in range(7):
            window = padded[
                :, row_off : row_off + num_rows, col_off : col_off + num_cols, :
            ].astype(jnp.float32)
            cols_out.append(jnp.sum(window * grad_float, axis=(0, 1, 2)))
        rows_out.append(jnp.stack(cols_out))
    return jnp.stack(rows_out)


def forward_tokens(depth_out, ln_gain, ln_bias, w_in, b_in, w_out, b_out):
    center = depth_out - jnp.mean(depth_out, axis=-1, keepdims=True)
    inv_std = lax.rsqrt(jnp.mean(center * center, axis=-1, keepdims=True) + 1e-06)
    norm_hat = center * inv_std
    normed = (norm_hat * ln_gain + ln_bias).astype(jnp.bfloat16)
    pre_act = jnp.dot(normed, w_in, preferred_element_type=jnp.float32) + b_in
    activated = jax.nn.gelu(pre_act, approximate=True).astype(jnp.bfloat16)
    branch = jnp.dot(activated, w_out, preferred_element_type=jnp.float32) + b_out
    return (norm_hat, inv_std, normed, pre_act, activated, branch)


def backward_tokens(masked, norm_hat, inv_std, pre_act, ln_gain, w_in, w_out, layer_scale):
    grad_branch = (masked * layer_scale).astype(jnp.bfloat16)
    grad_act = lax.dot_general(
        grad_branch, w_out, (((1,), (1,)), ((), ())), preferred_element_type=jnp.float32
    )
    unused, pull_back = jax.vjp(lambda v: jax.nn.gelu(v, approximate=True), pre_act)
    grad_pre = pull_back(grad_act)[0].astype(jnp.bfloat16)
    grad_norm = lax.dot_general(
        grad_pre, w_in, (((1,), (1,)), ((), ())), preferred_element_type=jnp.float32
    )
    scaled = grad_norm * ln_gain
    grad_depth = (
        inv_std
        * (
            scaled
            - jnp.mean(scaled, axis=-1, keepdims=True)
            - norm_hat * jnp.mean(scaled * norm_hat, axis=-1, keepdims=True)
        )
    ).astype(jnp.bfloat16)
    return (grad_branch, grad_pre, grad_norm, grad_depth)


def weight_terms(masked, branch, grad_branch, activated, normed, grad_pre, grad_norm, norm_hat):
    dims = (((0,), (0,)), ((), ()))
    grad_w_in = lax.dot_general(normed, grad_pre, dims, preferred_element_type=jnp.float32)
    grad_w_out = lax.dot_general(activated, grad_branch, dims, preferred_element_type=jnp.float32)
    return (
        grad_w_in,
        grad_w_out,
        jnp.sum(grad_pre.astype(jnp.float32), axis=0),
        jnp.sum(grad_branch.astype(jnp.float32), axis=0),
        jnp.sum(masked * branch, axis=0),
        jnp.sum(grad_norm * norm_hat, axis=0),
        jnp.sum(grad_norm, axis=0),
    )


def local(
    ocean_state,
    land_sea,
    cotangent,
    dw_kernel,
    dw_bias,
    ln_gain,
    ln_bias,
    w_in,
    b_in,
    w_out,
    b_out,
    layer_scale,
):
    num_batch, num_rows, num_cols, channels = ocean_state.shape
    mask_float = land_sea.astype(jnp.float32)[..., None]
    lon_ext = extended(ocean_state, (("lon", 2),), 3, True)
    padded = extended(lon_ext, (("lat", 1),), 3, False)
    depth_out = depthwise(padded, dw_kernel, num_rows, num_cols) + dw_bias
    masked = (mask_float * cotangent.astype(jnp.float32)).reshape(-1, channels)
    norm_hat, inv_std, normed, pre_act, activated, branch = forward_tokens(
        depth_out.reshape(-1, channels), ln_gain, ln_bias, w_in, b_in, w_out, b_out
    )
    grad_branch, grad_pre, grad_norm, grad_flat = backward_tokens(
        masked, norm_hat, inv_std, pre_act, ln_gain, w_in, w_out, layer_scale
    )
    grad_terms = weight_terms(
        masked, branch, grad_branch, activated, normed, grad_pre, grad_norm, norm_hat
    )
    grad_depth = grad_flat.reshape(num_batch, num_rows, num_cols, channels)
    grad_ext = extended(grad_depth, (("lon", 2),), 3, True)
    grad_pad = extended(grad_ext, (("lat", 1),), 3, False)
    branch_own = branch.reshape(num_batch, num_rows, num_cols, channels)
    output = (ocean_state.astype(jnp.float32) + mask_float * layer_scale * branch_own).astype(
        jnp.bfloat16
    )
    grad_state = (
        cotangent.astype(jnp.float32) + transposed(grad_pad, dw_kernel, num_rows, num_cols)
    ).astype(jnp.bfloat16)
    kernel_part = kernel_terms(padded, grad_depth, num_rows, num_cols)
    bias_part = jnp.sum(grad_depth.astype(jnp.float32), axis=(0, 1, 2))
    grad_w_in, grad_w_out, grad_b_in, grad_b_out, grad_scale, grad_ln_gain, grad_ln_bias = (
        grad_terms
    )
    reduced = lax.psum(
        (
            grad_w_in,
            grad_w_out,
            grad_b_in,
            grad_b_out,
            grad_scale,
            grad_ln_gain,
            grad_ln_bias,
            kernel_part,
            bias_part,
        ),
        ("lon", "lat"),
    )
    (
        grad_w_in,
        grad_w_out,
        grad_b_in,
        grad_b_out,
        grad_scale,
        grad_ln_gain,
        grad_ln_bias,
        kernel_part,
        bias_part,
    ) = reduced
    all_cells = num_batch * num_rows * num_cols * lax.axis_size("lon") * lax.axis_size("lat")
    factor = 1.0 / jnp.sqrt(jnp.float32(all_cells))
    return (
        output,
        grad_state,
        kernel_part * factor,
        bias_part * factor,
        grad_ln_gain * factor,
        grad_ln_bias * factor,
        grad_w_in * factor,
        grad_b_in * factor,
        grad_w_out * factor,
        grad_b_out * factor,
        grad_scale * factor,
    )


def solution(mesh):
    in_specs = (
        P(None, "lat", "lon", None),
        P(None, "lat", "lon"),
        P(None, "lat", "lon", None),
        P(),
        P(),
        P(),
        P(),
        P(),
        P(),
        P(),
        P(),
        P(),
    )
    out_specs = (
        P(None, "lat", "lon", None),
        P(None, "lat", "lon", None),
        P(),
        P(),
        P(),
        P(),
        P(),
        P(),
        P(),
        P(),
        P(),
    )
    return jax.shard_map(local, mesh=mesh, in_specs=in_specs, out_specs=out_specs, check_vma=False)
```

profile of v0, /device:TPU:0, one launch (start us, length us, event | category | flops | bytes accessed | tf_op | source)
XLA Modules:
  0.0 231.8 jit_solution(15919795681330468168)
XLA Ops:
  7.2 0.0 copy-start
  7.2 0.0 copy-start.1
  7.2 0.0 all-reduce.4.cloned.1.call-start
  7.3 0.8 fusion.147
  8.1 0.5 collective-permute-start.1
  8.6 0.1 collective-permute-start
  8.7 0.9 fusion.150
  9.6 1.0 fusion.148
  10.6 1.0 fusion.149
  11.7 0.9 constant_dynamic-update-slice_fusion.1
  12.6 0.7 convert_element_type.400
  13.3 0.0 collective-permute-done.1
  13.3 0.0 collective-permute-done
  13.3 1.0 pad_maximum_fusion.2
  14.3 4.8 %collective-permute-start.2 = (bf16[1,3,70,256]{3,2,1,0:T(8,128)(2,1)S(1)}, bf16[1,3,70,256]{3,2,1,0:T(8,128)(2,1)S(1)}, u32[]{:S(2)}, u32[]{:S(2)}) collective-permute-start(bf16[1,3,70,256]{3,2,1,0:T(8,128)(2,1)S(1)} %get-tuple-element.95), channel_id=1, source_target_pairs={{0,1},{1,2},{2,3},{3,4},{4,5},{5,6},{6,7},{7,8},{8,9},{9,10},{10,1... | collective-permute-start | bytes 322568 | tf_op jit(solution)/shard_map/ppermute | solution.py:14
  19.2 1.3 collective-permute-start.3
  20.5 1.2 collective-permute-done.2
  21.7 4.3 %collective-permute-done.3 = bf16[1,3,70,256]{3,2,1,0:T(8,128)(2,1)S(1)} collective-permute-done((bf16[1,3,70,256]{3,2,1,0:T(8,128)(2,1)S(1)}, bf16[1,3,70,256]{3,2,1,0:T(8,128)(2,1)S(1)}, u32[]{:S(2)}, u32[]{:S(2)}) %collective-permute-start.3) | collective-permute-done | bytes 107552 | tf_op jit(solution)/shard_map/ppermute | solution.py:15
  26.0 0.1 maximum_maximum_fusion
  26.1 0.0 copy-start.5
  26.1 0.0 copy-start.7
  26.1 0.0 copy-start.4
  26.2 3.2 %fusion.142 = (f32[6,64]{1,0:T(8,128)S(1)}, f32[1,6,64,256]{3,2,1,0:T(8,128)S(1)}) fusion(f32[256]{0:T(256)S(1)} %copy-done.8, f32[256]{0:T(256)S(1)} %bitcast.174, bf16[1,9,70,256]{3,2,1,0:T(8,128)(2,1)S(1)} %get-tuple-element.94, f32[256]{0:T(256)S(1)} %bitcast.176, f32[256]{0:T(256)S(1)} %bitcast.180, f32[256]{0:T(256)S(1)} %bitcast.182, ...), kind=kLoop, calls=%fused_computation.306 | loop fusion | flops 15433344 | bytes 9499136 | tf_op jit(solution)/shard_map/reduce_sum | solution.py:63
  29.3 0.1 div.15
  29.4 0.2 multiply_reduce_fusion.2
  29.6 0.1 rsqrt.12
  29.7 0.2 add_convert_fusion
  29.9 0.4 convolution_add_fusion
  30.3 0.1 copy-done.9
  30.4 0.6 convolution_add_fusion.1
  31.1 0.3 copy-done.3
  31.4 0.9 convert_reduce_fusion.1
  32.2 0.1 fusion.132
  32.3 1.3 convert_reduce_fusion
  33.6 0.5 multiply_reduce_fusion
  34.2 0.3 convert_reduce_fusion.2
  34.5 0.8 fusion.102
  35.2 0.8 fusion.130
  36.0 1.4 fusion.151
  37.4 1.7 fusion.141
  39.1 0.0 collective-permute-start.4
  39.1 0.5 collective-permute-start.5
  39.6 0.7 fusion.129
  40.6 43.3 %all-reduce = (f32[7,7,256]{2,1,0:T(8,128)S(1)}, f32[256]{0:T(256)S(1)}, f32[256]{0:T(256)S(1)}, f32[256]{0:T(256)S(1)}, f32[1024]{0:T(1024)S(1)}, /*index=5*/f32[256]{0:T(256)S(1)}, f32[256]{0:T(256)S(1)}) all-reduce(f32[7,7,256]{2,1,0:T(8,128)S(1)} %constant_dynamic-update-slice_fusion.2, ...), channel_id=1, replica_groups=mesh['lon'=2,'lat'=16] {'lon','lat'}, use_global_device_ids=true, to_apply=%region_53.0 | all-reduce | flops 14848 | bytes 118784 | tf_op jit(solution)/shard_map/psum | solution.py:154
  83.9 0.6 broadcast_multiply_fusion.2
  84.5 0.6 broadcast_multiply_fusion.11
  85.1 0.6 broadcast_multiply_fusion.10
  85.7 0.6 broadcast_multiply_fusion.9
  86.2 0.6 broadcast_multiply_fusion.3
  86.8 0.6 broadcast_multiply_fusion.8
  87.4 0.0 all-reduce.4.cloned.1.call-update
  87.4 0.0 collective-permute-done.4
  87.4 0.0 collective-permute-done.5
  87.4 0.1 pad_maximum_fusion.3
  87.5 1.3 collective-permute-start.6
  88.8 4.8 %collective-permute-start.7 = (bf16[1,3,70,256]{3,2,1,0:T(8,128)(2,1)S(1)}, bf16[1,3,70,256]{3,2,1,0:T(8,128)(2,1)S(1)}, u32[]{:S(2)}, u32[]{:S(2)}) collective-permute-start(bf16[1,3,70,256]{3,2,1,0:T(8,128)(2,1)S(1)} %get-tuple-element.92), channel_id=1, source_target_pairs={{0,1},{1,2},{2,3},{3,4},{4,5},{5,6},{6,7},{7,8},{8,9},{9,10},{10,1... | collective-permute-start | bytes 322568 | tf_op jit(solution)/shard_map/ppermute | solution.py:14
  93.6 0.6 broadcast_multiply_fusion.7
  94.2 0.2 collective-permute-done.6
  94.4 4.7 %collective-permute-done.7 = bf16[1,3,70,256]{3,2,1,0:T(8,128)(2,1)S(1)} collective-permute-done((bf16[1,3,70,256]{3,2,1,0:T(8,128)(2,1)S(1)}, bf16[1,3,70,256]{3,2,1,0:T(8,128)(2,1)S(1)}, u32[]{:S(2)}, u32[]{:S(2)}) %collective-permute-start.7) | collective-permute-done | bytes 107552 | tf_op jit(solution)/shard_map/ppermute | solution.py:14
  99.2 0.1 pad_maximum_fusion.1
  99.2 3.8 %fusion.55 = bf16[1,6,64,256]{3,2,1,0:T(8,128)(2,1)} fusion(bf16[1,6,64,256]{3,2,1,0:T(8,128)(2,1)S(1)} %copy-done.3, bf16[1,6,64,256]{3,2,1,0:T(8,128)(2,1)S(1)} %bitcast.153, bf16[1,6,3,256]{3,2,1,0:T(4,128)(2,1)S(1)} %collective-permute-done.4, bf16[1,6,3,256]{3,2,1,0:T(4,128)(2,1)S(1)} %collective-permute-done.5, ...), kind=kLoop, calls=%fused_computation.165 | loop fusion | flops 16416768 | bytes 8915968 | tf_op jit(solution)/shard_map/convert_element_type | solution.py:148
  103.0 118.4 %all-reduce.4.cloned.1.call-done = (f32[256,1024]{1,0:T(8,128)}, f32[1024,256]{1,0:T(8,128)}) async-done(((f32[256,1024]{1,0:T(8,128)}, f32[1024,256]{1,0:T(8,128)}), (f32[256,1024]{1,0:T(8,128)}, f32[1024,256]{1,0:T(8,128)})) %all-reduce.4.cloned.1.call-update) | async-done | bytes 2097168 | tf_op jit(solution)/shard_map/psum | solution.py:154
  221.4 2.4 %broadcast_multiply_fusion.1 = f32[256,1024]{1,0:T(8,128)} fusion(f32[256,1024]{1,0:T(8,128)} %get-tuple-element.81), kind=kLoop, calls=%fused_computation.66 | loop fusion | flops 262144 | bytes 2097152 | tf_op jit(solution)/shard_map/mul | solution.py:188
  223.8 1.1 broadcast_multiply_fusion
  (37 shorter events, 0.3 us)
Async XLA Ops:
  7.2 22.7 %copy-start = (bf16[256,1024]{1,0:T(8,128)(2,1)S(1)}, bf16[256,1024]{1,0:T(8,128)(2,1)}, u32[]{:S(2)}) copy-start(bf16[256,1024]{1,0:T(8,128)(2,1)} %param.19) | copy-start | bytes 1572868
  7.2 18.8 %copy-start.1 = (bf16[1,6,64,256]{3,2,1,0:T(8,128)(2,1)S(1)}, bf16[1,6,64,256]{3,2,1,0:T(8,128)(2,1)}, u32[]{:S(2)}) copy-start(bf16[1,6,64,256]{3,2,1,0:T(8,128)(2,1)} %param.12) | copy-start | bytes 589828
  7.2 18.9 %copy-start.8 = (f32[256]{0:T(256)S(1)}, f32[256]{0:T(256)}, u32[]{:S(2)}) copy-start(f32[256]{0:T(256)} %param.16) | copy-start | bytes 3076
  7.2 214.2 %all-reduce.4.cloned.1.call-start = ((), (), s32[]{:S(2)}) async-start(), calls=%async_computation | async-start | bytes 4194304 | tf_op jit(solution)/shard_map/psum | solution.py:154
  8.1 5.2 %collective-permute-start.1 = (bf16[1,6,3,256]{3,2,1,0:T(4,128)(2,1)S(1)}, bf16[1,6,3,256]{3,2,1,0:T(4,128)(2,1)S(1)}, u32[]{:S(2)}, u32[]{:S(2)}) collective-permute-start(bf16[1,6,3,256]{3,2,1,0:T(4,128)(2,1)S(1)} %get-tuple-element.102), channel_id=1, source_target_pairs={{16,0},{0,16},{17,1},{1,17},{18,2},{2,18},{19,3},{3,19},{20,4},{4,... | collective-permute-start | bytes 27656 | tf_op jit(solution)/shard_map/ppermute | solution.py:15
  8.6 4.7 %collective-permute-start = (bf16[1,6,3,256]{3,2,1,0:T(4,128)(2,1)S(1)}, bf16[1,6,3,256]{3,2,1,0:T(4,128)(2,1)S(1)}, u32[]{:S(2)}, u32[]{:S(2)}) collective-permute-start(bf16[1,6,3,256]{3,2,1,0:T(4,128)(2,1)S(1)} %get-tuple-element.101), channel_id=1, source_target_pairs={{0,16},{16,0},{1,17},{17,1},{2,18},{18,2},{3,19},{19,3},{4,20},{20... | collective-permute-start | bytes 27656 | tf_op jit(solution)/shard_map/ppermute | solution.py:14
  14.3 7.4 %collective-permute-start.2 = (bf16[1,3,70,256]{3,2,1,0:T(8,128)(2,1)S(1)}, bf16[1,3,70,256]{3,2,1,0:T(8,128)(2,1)S(1)}, u32[]{:S(2)}, u32[]{:S(2)}) collective-permute-start(bf16[1,3,70,256]{3,2,1,0:T(8,128)(2,1)S(1)} %get-tuple-element.95), channel_id=1, source_target_pairs={{0,1},{1,2},{2,3},{3,4},{4,5},{5,6},{6,7},{7,8},{8,9},{9,10},{10,1... | collective-permute-start | bytes 322568 | tf_op jit(solution)/shard_map/ppermute | solution.py:14
  19.2 6.9 %collective-permute-start.3 = (bf16[1,3,70,256]{3,2,1,0:T(8,128)(2,1)S(1)}, bf16[1,3,70,256]{3,2,1,0:T(8,128)(2,1)S(1)}, u32[]{:S(2)}, u32[]{:S(2)}) collective-permute-start(bf16[1,3,70,256]{3,2,1,0:T(8,128)(2,1)S(1)} %get-tuple-element.96), channel_id=1, source_target_pairs={{1,0},{2,1},{3,2},{4,3},{5,4},{6,5},{7,6},{8,7},{9,8},{10,9},{11,1... | collective-permute-start | bytes 322568 | tf_op jit(solution)/shard_map/ppermute | solution.py:15
  26.1 3.6 %copy-start.5 = (f32[256]{0:T(256)S(1)}, f32[256]{0:T(256)}, u32[]{:S(2)}) copy-start(f32[256]{0:T(256)} %param.17) | copy-start | bytes 3076
  26.1 3.6 %copy-start.7 = (f32[256]{0:T(256)S(1)}, f32[256]{0:T(256)}, u32[]{:S(2)}) copy-start(f32[256]{0:T(256)} %param.18) | copy-start | bytes 3076
  26.1 3.8 %copy-start.4 = (f32[1024]{0:T(1024)S(1)}, f32[1024]{0:T(1024)}, u32[]{:S(2)}) copy-start(f32[1024]{0:T(1024)} %param.20) | copy-start | bytes 12292
  29.4 1.0 copy-start.9
  29.4 1.0 copy-start.10
  30.4 0.9 copy-start.3
  30.4 0.9 copy-start.6
  39.1 48.3 %collective-permute-start.4 = (bf16[1,6,3,256]{3,2,1,0:T(4,128)(2,1)S(1)}, bf16[1,6,3,256]{3,2,1,0:T(4,128)(2,1)S(1)}, u32[]{:S(2)}, u32[]{:S(2)}) collective-permute-start(bf16[1,6,3,256]{3,2,1,0:T(4,128)(2,1)S(1)} %get-tuple-element.100), channel_id=1, source_target_pairs={{0,16},{16,0},{1,17},{17,1},{2,18},{18,2},{3,19},{19,3},{4,20},{20... | collective-permute-start | bytes 27656 | tf_op jit(solution)/shard_map/ppermute | solution.py:14
  39.1 48.3 %collective-permute-start.5 = (bf16[1,6,3,256]{3,2,1,0:T(4,128)(2,1)S(1)}, bf16[1,6,3,256]{3,2,1,0:T(4,128)(2,1)S(1)}, u32[]{:S(2)}, u32[]{:S(2)}) collective-permute-start(bf16[1,6,3,256]{3,2,1,0:T(4,128)(2,1)S(1)} %get-tuple-element.99), channel_id=1, source_target_pairs={{16,0},{0,16},{17,1},{1,17},{18,2},{2,18},{19,3},{3,19},{20,4},{4,... | collective-permute-start | bytes 27656 | tf_op jit(solution)/shard_map/ppermute | solution.py:15
  87.5 6.9 %collective-permute-start.6 = (bf16[1,3,70,256]{3,2,1,0:T(8,128)(2,1)S(1)}, bf16[1,3,70,256]{3,2,1,0:T(8,128)(2,1)S(1)}, u32[]{:S(2)}, u32[]{:S(2)}) collective-permute-start(bf16[1,3,70,256]{3,2,1,0:T(8,128)(2,1)S(1)} %get-tuple-element.91), channel_id=1, source_target_pairs={{1,0},{2,1},{3,2},{4,3},{5,4},{6,5},{7,6},{8,7},{9,8},{10,9},{11,1... | collective-permute-start | bytes 322568 | tf_op jit(solution)/shard_map/ppermute | solution.py:15
  88.8 10.3 %collective-permute-start.7 = (bf16[1,3,70,256]{3,2,1,0:T(8,128)(2,1)S(1)}, bf16[1,3,70,256]{3,2,1,0:T(8,128)(2,1)S(1)}, u32[]{:S(2)}, u32[]{:S(2)}) collective-permute-start(bf16[1,3,70,256]{3,2,1,0:T(8,128)(2,1)S(1)} %get-tuple-element.92), channel_id=1, source_target_pairs={{0,1},{1,2},{2,3},{3,4},{4,5},{5,6},{6,7},{7,8},{8,9},{9,10},{10,1... | collective-permute-start | bytes 322568 | tf_op jit(solution)/shard_map/ppermute | solution.py:14
  221.4 2.4 %copy-start.2 = (f32[1024,256]{1,0:T(8,128)S(1)}, f32[1024,256]{1,0:T(8,128)}, u32[]{:S(2)}) copy-start(f32[1024,256]{1,0:T(8,128)} %get-tuple-element.82) | copy-start | bytes 3145732
Sparse Core Ops, SparseCore 0:
  87.5 133.8 all-reduce.3
where the time goes:
time: 232 us
  waiting for transfers between devices  129 us (56%)
  blocking collectives  43.3 us (19%)
  other arithmetic  20.3 us (9%)
  between operations  14.3 us (6%)
  starting transfers between devices  13.4 us (6%)
  matrix products  5.94 us (3%)
  local copies, waits for them, and re-layouts  5.64 us (2%)
    psum x1, waiting for transfers between devices, local(): lax.psum((grad_w_in, grad_w_out, grad_b_in, grad_b_out, grad_scale, grad_...  118 us
    psum x1, blocking collectives, local(): lax.psum((grad_w_in, grad_w_out, grad_b_in, grad_b_out, grad_scale, grad_...  43.3 us
    ppermute x4, starting transfers between devices, extended(): before = lax.ppermute(last, axis, up)  9.72 us
    ppermute x4, waiting for transfers between devices, extended(): before = lax.ppermute(last, axis, up)  5.94 us
  transfers between devices with their start and end apart: 9, of which 5 were waited for; matrix products, arithmetic and copies ran while one was open for 6% of the time, Pallas kernels for 0%

commit v1 on v0

--- a/solution.py
+++ b/solution.py
@@ -1,7 +1,227 @@
+import functools
 import jax
 import jax.numpy as jnp
 from jax import lax
+from jax.experimental import pallas as pl
+from jax.experimental.pallas import tpu as pltpu
 from jax.sharding import PartitionSpec as P
+
+MESH = pl.DeviceIdType.MESH
+
+
+def phases_of(num_lon, num_lat):
+    phases = []
+    for axis, size in (("lon", num_lon), ("lat", num_lat)):
+        stride = 1
+        while stride < size:
+            rest = size // stride
+            if axis == "lon" and stride == 1 and rest % 2 == 0:
+                count = 2
+            elif rest % 4 == 0:
+                count = 4
+            elif rest % 2 == 0:
+                count = 2
+            else:
+                count = rest
+            phases.append((axis, stride, count))
+            stride *= count
+    return phases
+
+
+def plan(rows, tile, phases):
+    steps = []
+    for axis, stride, count in phases:
+        scatter = rows % (count * tile) == 0
+        steps.append((axis, stride, count, scatter, rows))
+        if scatter:
+            rows //= count
+    return steps, rows
+
+
+def position(axis, stride, count):
+    index = lax.axis_index(axis)
+    return index, lax.rem(lax.div(index, stride), count)
+
+
+def partner(axis, stride, count, k):
+    index, digit = position(axis, stride, count)
+    other = lax.rem(digit + k, count)
+    return {axis: index + (other - digit) * stride}, other
+
+
+class Reducer:
+    def __init__(self, tile, steps, mine, whole, landing, send_sem, recv_sem, back_send, back_recv):
+        self.tile, self.steps = tile, steps
+        self.mine, self.whole, self.landing = mine, whole, landing
+        self.send_sem, self.recv_sem = send_sem, recv_sem
+        self.back_send, self.back_recv = back_send, back_recv
+        self.offsets = [0]
+        for axis, stride, count, scatter, rows in steps:
+            digit = position(axis, stride, count)[1]
+            step = digit * (rows // count) if scatter else 0
+            self.offsets.append(self.offsets[-1] + step)
+
+    def span(self, start, rows):
+        return pl.ds(pl.multiple_of(start, self.tile), rows)
+
+    def scatter_copies(self, number):
+        axis, stride, count, scatter, rows = self.steps[number]
+        copies = []
+        part = rows // count if scatter else rows
+        for k in range(1, count):
+            device, other = partner(axis, stride, count, k)
+            start = self.offsets[number] + (other * part if scatter else 0)
+            copies.append(
+                pltpu.make_async_remote_copy(
+                    src_ref=self.mine.at[self.span(start, part)],
+                    dst_ref=self.landing[number].at[k],
+                    send_sem=self.send_sem.at[number, k],
+                    recv_sem=self.recv_sem.at[number, k],
+                    device_id=device,
+                    device_id_type=MESH,
+                )
+            )
+        return copies
+
+    def scatter_start(self, number):
+        for copy in self.scatter_copies(number):
+            copy.start()
+
+    def scatter_finish(self, number, last):
+        axis, stride, count, scatter, rows = self.steps[number]
+        digit = position(axis, stride, count)[1]
+        for copy in self.scatter_copies(number):
+            copy.wait()
+        part = rows // count if scatter else rows
+        here = self.span(self.offsets[number + 1], part)
+        land = self.landing[number]
+        if scatter:
+            total = self.mine[here].astype(jnp.float32)
+            for k in range(1, count):
+                total = total + land[k].astype(jnp.float32)
+        else:
+            land[0] = self.mine[here]
+            total = land[digit].astype(jnp.float32)
+            for j in range(1, count):
+                total = total + land[lax.rem(digit - j + count, count)].astype(jnp.float32)
+        target = self.whole if last else self.mine
+        target[here] = total.astype(target.dtype)
+
+    def gather_copies(self, number):
+        axis, stride, count, scatter, rows = self.steps[number]
+        part = rows // count
+        here = self.span(self.offsets[number + 1], part)
+        copies = []
+        for k in range(1, count):
+            device, other = partner(axis, stride, count, k)
+            copies.append(
+                pltpu.make_async_remote_copy(
+                    src_ref=self.whole.at[here],
+                    dst_ref=self.whole.at[here],
+                    send_sem=self.back_send.at[number, k],
+                    recv_sem=self.back_recv.at[number, k],
+                    device_id=device,
+                    device_id_type=MESH,
+                )
+            )
+        return copies
+
+    def gather_start(self, number):
+        if self.steps[number][3]:
+            for copy in self.gather_copies(number):
+                copy.start()
+
+    def gather_finish(self, number):
+        if self.steps[number][3]:
+            for copy in self.gather_copies(number):
+                copy.wait()
+
+
+def greet(phases):
+    barrier = pltpu.get_barrier_semaphore()
+    total = 0
+    for axis, stride, count in phases:
+        for k in range(1, count):
+            device, _ = partner(axis, stride, count, k)
+            pl.semaphore_signal(barrier, inc=1, device_id=device, device_id_type=MESH)
+            total += 1
+    pl.semaphore_wait(barrier, total)
+
+
+def sum_kernel(phases, steps, small_steps, wide_ref, tall_ref, small_ref, wide_out, tall_out, small_out, *scratch):
+    num = len(phases)
+    mine, whole, small_whole = scratch[:3]
+    landing = scratch[3 : 3 + num]
+    small_landing = scratch[3 + num : 3 + 2 * num]
+    sems = scratch[3 + 2 * num :]
+    channels = tall_ref.shape[1]
+    depth = wide_ref.shape[0]
+    tall = tall_ref.shape[0]
+    blocks = wide_ref.shape[1] // channels
+    greet(phases)
+    mine[0:tall] = tall_ref[...]
+    for b in range(blocks):
+        mine[tall + b * depth : tall + (b + 1) * depth] = wide_ref[:, b * channels : (b + 1) * channels]
+    big = Reducer(16, steps, mine, whole, landing, *sems[:4])
+    small = Reducer(8, small_steps, small_ref, small_whole, small_landing, *sems[4:])
+    for number in range(num):
+        big.scatter_start(number)
+        small.scatter_start(number)
+        small.scatter_finish(number, number == num - 1)
+        big.scatter_finish(number, number == num - 1)
+    for number in reversed(range(num)):
+        big.gather_start(number)
+        small.gather_start(number)
+        small.gather_finish(number)
+        big.gather_finish(number)
+    small_out[...] = small_whole[...]
+    tall_out[...] = whole[0:tall]
+    for b in range(blocks):
+        wide_out[:, b * channels : (b + 1) * channels] = whole[tall + b * depth : tall + (b + 1) * depth]
+
+
+def summed_over_devices(wide, tall, small):
+    phases = phases_of(lax.axis_size("lon"), lax.axis_size("lat"))
+    num = len(phases)
+    channels = tall.shape[1]
+    rows = tall.shape[0] + wide.shape[1] // channels * wide.shape[0]
+    steps, _ = plan(rows, 16, phases)
+    small_steps, _ = plan(small.shape[0], 8, phases)
+
+    def landings(which, dtype):
+        return [
+            pltpu.VMEM((count, r // count if scatter else r, channels), dtype)
+            for axis, stride, count, scatter, r in which
+        ]
+
+    vmem = pl.BlockSpec(memory_space=pltpu.VMEM)
+
+    def body(wide_ref, tall_ref, small_ref, wide_out, tall_out, small_out, small_mine, *scratch):
+        small_mine[...] = small_ref[...]
+        sum_kernel(phases, steps, small_steps, wide_ref, tall_ref, small_mine, wide_out, tall_out, small_out, *scratch)
+
+    return pl.pallas_call(
+        body,
+        out_shape=(
+            jax.ShapeDtypeStruct(wide.shape, jnp.bfloat16),
+            jax.ShapeDtypeStruct(tall.shape, jnp.bfloat16),
+            jax.ShapeDtypeStruct(small.shape, jnp.float32),
+        ),
+        in_specs=[vmem] * 3,
+        out_specs=(vmem,) * 3,
+        scratch_shapes=[
+            pltpu.VMEM(small.shape, jnp.float32),
+            pltpu.VMEM((rows, channels), jnp.bfloat16),
+            pltpu.VMEM((rows, channels), jnp.bfloat16),
+            pltpu.VMEM(small.shape, jnp.float32),
+            *landings(steps, jnp.bfloat16),
+            *landings(small_steps, jnp.float32),
+            *[pltpu.SemaphoreType.DMA((num, 4))] * 8,
+        ],
+        compiler_params=pltpu.CompilerParams(
+            collective_id=0, has_side_effects=True, vmem_limit_bytes=40 * 1024 * 1024
+        ),
+    )(wide, tall, small)
 
 
 def extended(array, sides, width, wrap):
@@ -151,45 +371,36 @@
     grad_w_in, grad_w_out, grad_b_in, grad_b_out, grad_scale, grad_ln_gain, grad_ln_bias = (
         grad_terms
     )
-    reduced = lax.psum(
-        (
-            grad_w_in,
-            grad_w_out,
-            grad_b_in,
-            grad_b_out,
-            grad_scale,
-            grad_ln_gain,
-            grad_ln_bias,
-            kernel_part,
-            bias_part,
-        ),
-        ("lon", "lat"),
-    )
-    (
-        grad_w_in,
-        grad_w_out,
-        grad_b_in,
-        grad_b_out,
-        grad_scale,
-        grad_ln_gain,
-        grad_ln_bias,
-        kernel_part,
-        bias_part,
-    ) = reduced
+    rows = [
+        kernel_part.reshape(-1, channels),
+        bias_part[None],
+        grad_ln_gain[None],
+        grad_ln_bias[None],
+        grad_b_out[None],
+        grad_scale[None],
+        grad_b_in.reshape(-1, channels),
+    ]
+    used = sum(r.shape[0] for r in rows)
+    small = jnp.concatenate(rows + [jnp.zeros((-used % 64, channels), jnp.float32)])
+    grad_w_in, grad_w_out, small = summed_over_devices(
+        grad_w_in.astype(jnp.bfloat16), grad_w_out.astype(jnp.bfloat16), small
+    )
+    grad_w_in, grad_w_out = (grad_w_in.astype(jnp.float32), grad_w_out.astype(jnp.float32))
     all_cells = num_batch * num_rows * num_cols * lax.axis_size("lon") * lax.axis_size("lat")
     factor = 1.0 / jnp.sqrt(jnp.float32(all_cells))
+    small = small * factor
     return (
         output,
         grad_state,
-        kernel_part * factor,
-        bias_part * factor,
-        grad_ln_gain * factor,
-        grad_ln_bias * factor,
+        small[:49].reshape(7, 7, channels),
+        small[49],
+        small[50],
+        small[51],
         grad_w_in * factor,
-        grad_b_in * factor,
+        small[54 : 54 + b_in.shape[0] // channels].reshape(-1),
         grad_w_out * factor,
-        grad_b_out * factor,
-        grad_scale * factor,
+        small[52],
+        small[53],
     )
 
 

time: 232 us -> 88.5 us (0.38)
  waiting for transfers between devices: 129 us -> 7.34 us
  blocking collectives: 43.3 us -> 0 us
  Pallas kernels: 0 us -> 34 us
  between operations: 14.3 us -> 1.9 us
  other arithmetic: 20.3 us -> 16.6 us
    psum x1 -> x0, waiting for transfers between devices: 118 us -> none  [local(): lax.psum((grad_w_in, grad_w_out, grad_b_in, grad_b_out, grad_scale, grad_...]
    psum x1 -> x0, blocking collectives: 43.3 us -> none  [local(): lax.psum((grad_w_in, grad_w_out, grad_b_in, grad_b_out, grad_scale, grad_...]
    pallas_call x0 -> x1, Pallas kernels: none -> 34 us  [summed_over_devices(): pl.pallas_call(body, out_shape=(jax.ShapeDtypeStruct(wide.shape, jnp.bflo...]
    mul x7 -> x1, other arithmetic: 4.04 us -> 0.01 us  [local(): small = small * factor]
    ppermute x4, waiting for transfers between devices: 5.94 us -> 2.92 us  [extended(): before = lax.ppermute(last, axis, up)]
  transfers between devices with their start and end apart: 9 -> 8, of which waited for: 5 -> 4; matrix products, arithmetic and copies ran while one was open for 6% -> 11% of each run, Pallas kernels for 0% -> 39%
where the time goes in v1:
time: 88.5 us; the launch traced here: 86.9 us
  Pallas kernels  34 us (38%)
  other arithmetic  16.6 us (19%)
  starting transfers between devices  13.1 us (15%)
  local copies, waits for them, and re-layouts  7.76 us (9%)
  waiting for transfers between devices  7.34 us (8%)
  matrix products  6.16 us (7%)
  between operations  1.9 us (2%)
    pallas_call x1, Pallas kernels, summed_over_devices(): pl.pallas_call(body, out_shape=(jax.ShapeDtypeStruct(wide.shape, jnp.bflo...  34 us
    ppermute x4, starting transfers between devices, extended(): before = lax.ppermute(last, axis, up)  10.4 us
    ppermute x4, waiting for transfers between devices, extended(): after = lax.ppermute(leading, axis, down)  4.42 us
    convert_element_type x1, other arithmetic, local(): grad_state = (cotangent.astype(jnp.float32) + transposed(grad_pad, dw_ker...  3.77 us
    reduce_sum x1, other arithmetic, forward_tokens(): center = depth_out - jnp.mean(depth_out, axis=-1, keepdims=True)  3.15 us
    slice x3, local copies, waits for them, and re-layouts, depthwise(): kernel[row_off, col_off]  2.92 us
    ppermute x4, waiting for transfers between devices, extended(): before = lax.ppermute(last, axis, up)  2.92 us
    ppermute x4, starting transfers between devices, extended(): after = lax.ppermute(leading, axis, down)  2.73 us
  transfers between devices with their start and end apart: 8, of which 4 were waited for; matrix products, arithmetic and copies ran while one was open for 11% of the time, Pallas kernels for 39%

profile of v1, /device:TPU:0, one launch (start us, length us, event | category | flops | bytes accessed | tf_op | source)
XLA Modules:
  0.0 86.9 jit_solution(18313868762154165018)
XLA Ops:
  0.6 0.0 copy-start
  0.7 0.0 copy-start.1
  0.7 0.8 fusion.146
  1.5 0.5 collective-permute-start
  2.0 0.1 collective-permute-start.1
  2.1 0.9 %fusion.150 = (f32[1,1,256]{2,1,0:T(1,128)S(1)}, f32[1,1,256]{2,1,0:T(1,128)S(1)}, f32[1,1,256]{2,1,0:T(1,128)S(1)}, f32[1,1,256]{2,1,0:T(1,128)S(1)}, f32[1,1,2...) fusion(f32[7,7,256]{2,1,0:T(8,128)} %param.15), kind=kLoop, calls=%fused_computation.310 | loop fusion | bytes 22528 | tf_op jit(solution)/shard_map/slice | solution.py:249
  3.0 1.0 %fusion.148 = (f32[1,1,256]{2,1,0:T(1,128)S(1)}, f32[1,1,256]{2,1,0:T(1,128)S(1)}, f32[1,1,256]{2,1,0:T(1,128)S(1)}, f32[1,1,256]{2,1,0:T(1,128)S(1)}, f32[1,1,2...) fusion(f32[7,7,256]{2,1,0:T(8,128)} %param.15), kind=kLoop, calls=%fused_computation.308 | loop fusion | bytes 38912 | tf_op jit(solution)/shard_map/slice | solution.py:249
  4.0 0.0 copy-start.3
  4.1 1.0 %fusion.149 = (f32[1,1,256]{2,1,0:T(1,128)S(1)}, f32[1,1,256]{2,1,0:T(1,128)S(1)}, f32[1,1,256]{2,1,0:T(1,128)S(1)}, f32[1,1,256]{2,1,0:T(1,128)S(1)}, f32[1,1,2...) fusion(f32[7,7,256]{2,1,0:T(8,128)} %param.15), kind=kLoop, calls=%fused_computation.309 | loop fusion | bytes 38912 | tf_op jit(solution)/shard_map/slice | solution.py:249
  5.3 0.9 %constant_dynamic-update-slice_fusion.1 = bf16[1,6,67,256]{3,2,1,0:T(8,128)(2,1)S(1)} fusion(bf16[1,6,64,256]{3,2,1,0:T(8,128)(2,1)} %param.12), kind=kLoop, calls=%fused_computation.288 | loop fusion | bytes 393216
  6.3 0.7 convert_element_type.412
  7.0 0.0 collective-permute-done
  7.0 0.0 collective-permute-done.1
  7.0 1.0 %pad_maximum_fusion.2 = bf16[1,6,70,256]{3,2,1,0:T(8,128)(2,1)S(1)} fusion(bf16[1,6,3,256]{3,2,1,0:T(4,128)(2,1)S(1)} %collective-permute-done.1, bf16[1,6,64,256]{3,2,1,0:T(8,128)(2,1)} %param.12, bf16[1,6,3,256]{3,2,1,0:T(4,128)(2,1)S(1)} %collective-permute-done), kind=kLoop, calls=%fused_computation.269 | loop fusion | flops 645120 | bytes 430080 | tf_op jit(solution)/shard_map/concatenate | solution.py:236
  8.0 4.8 %collective-permute-start.2 = (bf16[1,3,70,256]{3,2,1,0:T(8,128)(2,1)S(1)}, bf16[1,3,70,256]{3,2,1,0:T(8,128)(2,1)S(1)}, u32[]{:S(2)}, u32[]{:S(2)}) collective-permute-start(bf16[1,3,70,256]{3,2,1,0:T(8,128)(2,1)S(1)} %get-tuple-element.92), channel_id=1, source_target_pairs={{0,1},{1,2},{2,3},{3,4},{4,5},{5,6},{6,7},{7,8},{8,9},{9,10},{10,1... | collective-permute-start | bytes 322568 | tf_op jit(solution)/shard_map/ppermute | solution.py:234
  12.8 1.3 %collective-permute-start.3 = (bf16[1,3,70,256]{3,2,1,0:T(8,128)(2,1)S(1)}, bf16[1,3,70,256]{3,2,1,0:T(8,128)(2,1)S(1)}, u32[]{:S(2)}, u32[]{:S(2)}) collective-permute-start(bf16[1,3,70,256]{3,2,1,0:T(8,128)(2,1)S(1)} %get-tuple-element.93), channel_id=1, source_target_pairs={{1,0},{2,1},{3,2},{4,3},{5,4},{6,5},{7,6},{8,7},{9,8},{10,9},{11,1... | collective-permute-start | bytes 322568 | tf_op jit(solution)/shard_map/ppermute | solution.py:235
  14.1 1.2 %collective-permute-done.2 = bf16[1,3,70,256]{3,2,1,0:T(8,128)(2,1)S(1)} collective-permute-done((bf16[1,3,70,256]{3,2,1,0:T(8,128)(2,1)S(1)}, bf16[1,3,70,256]{3,2,1,0:T(8,128)(2,1)S(1)}, u32[]{:S(2)}, u32[]{:S(2)}) %collective-permute-start.2) | collective-permute-done | bytes 107552 | tf_op jit(solution)/shard_map/ppermute | solution.py:234
  15.4 4.3 %collective-permute-done.3 = bf16[1,3,70,256]{3,2,1,0:T(8,128)(2,1)S(1)} collective-permute-done((bf16[1,3,70,256]{3,2,1,0:T(8,128)(2,1)S(1)}, bf16[1,3,70,256]{3,2,1,0:T(8,128)(2,1)S(1)}, u32[]{:S(2)}, u32[]{:S(2)}) %collective-permute-start.3) | collective-permute-done | bytes 107552 | tf_op jit(solution)/shard_map/ppermute | solution.py:235
  19.7 0.1 maximum_maximum_fusion
  19.8 0.0 copy-start.57
  19.8 0.0 copy-start.63
  19.8 0.0 copy-start.55
  19.8 3.1 %fusion.141 = (f32[6,64]{1,0:T(8,128)S(1)}, f32[1,6,64,256]{3,2,1,0:T(8,128)S(1)}) fusion(f32[256]{0:T(256)S(1)} %copy-done.66, f32[256]{0:T(256)S(1)} %bitcast.187, bf16[1,9,70,256]{3,2,1,0:T(8,128)(2,1)S(1)} %get-tuple-element.91, f32[256]{0:T(256)S(1)} %bitcast.189, f32[256]{0:T(256)S(1)} %bitcast.193, f32[256]{0:T(256)S(1)} %bitcast.195, ...), kind=kLoop, calls=%fused_computation.302 | loop fusion | flops 15433344 | bytes 9499136 | tf_op jit(solution)/shard_map/reduce_sum | solution.py:283
  23.2 0.1 div.15
  23.3 0.2 multiply_reduce_fusion.2
  23.5 0.1 rsqrt.12
  23.6 0.2 add_convert_fusion
  23.8 0.4 convolution_add_fusion
  24.2 0.0 copy-start.2
  24.2 0.0 copy-start.62
  24.2 1.7 %convolution_add_fusion.1 = f32[384,256]{1,0:T(8,128)S(1)} fusion(bf16[1024,256]{1,0:T(8,128)(2,1)} %param.21, f32[256]{0:T(256)S(1)} %copy-done.68, f32[384,1024]{1,0:T(8,128)S(1)} %convolution_add_fusion), kind=kOutput, calls=%fused_computation.64 | convolution fusion | flops 204963840 | bytes 2491392 | tf_op jit(solution)/shard_map/dot_general | solution.py:289
  26.0 1.4 %convert_reduce_fusion.1 = (f32[256]{0:T(256)}, f32[1,6,64,256]{3,2,1,0:T(8,128)S(1)}, bf16[1,6,64,256]{3,2,1,0:T(8,128)(2,1)}) fusion(f32[256]{0:T(256)S(1)} %copy-done.62, bf16[1,6,64,256]{3,2,1,0:T(8,128)(2,1)S(1)} %copy-done.2, f32[6,64]{1,0:T(8,128)S(1)} %bitcast.168, f32[1,6,64,256]{3,2,1,0:T(8,128)S(1)} %bitcast.167, ...), kind=kLoop, calls=%fused_computation.249 | loop fusion | flops 1081088 | bytes 1379840 | tf_op jit(solution)/shard_map/reduce_sum | solution.py:323
  27.4 0.6 fusion.132
  28.0 0.7 convolution_convert_fusion.tall_ref
  28.7 0.3 copy-done.67
  29.1 1.9 %convert_reduce_fusion = (f32[1024]{0:T(1024)}, bf16[384,1024]{1,0:T(8,128)(2,1)S(1)}) fusion(f32[384,1024]{1,0:T(8,128)S(1)} %convolution_add_fusion, bf16[384,256]{1,0:T(8,128)(2,1)S(1)} %get-tuple-element.85, bf16[1024,256]{1,0:T(8,128)(2,1)S(1)} %copy-done.67), kind=kOutput, calls=%fused_computation.59 | convolution fusion | flops 209976320 | bytes 3084288 | tf_op jit(solution)/shard_map/dot_general | solution.py:295
  30.9 0.5 convolution_convert_fusion.1.wide_ref
  31.4 1.1 %multiply_reduce_fusion = (f32[256]{0:T(256)}, f32[384]{0:T(512)S(1)}, f32[384]{0:T(512)S(1)}, f32[256]{0:T(256)}, f32[384,256]{1,0:T(8,128)S(1)}) fusion(f32[1,6,64,256]{3,2,1,0:T(8,128)S(1)} %get-tuple-element.83, f32[384]{0:T(512)S(1)} %rsqrt.12, f32[384]{0:T(512)S(1)} %div.15, f32[256]{0:T(256)S(1)} %copy-done.58, ...), kind=kOutput, calls=%fused_computation.251 | convolution fusion | flops 202210048 | bytes 2106368 | tf_op jit(solution)/shard_map/dot_general | solution.py:300
  32.5 0.9 convert_reduce_fusion.2
  33.3 0.8 fusion.102
  34.1 0.8 fusion.130
  34.9 0.0 copy-start.60
  34.9 0.0 copy-start.61
  34.9 0.0 copy-start.64
  34.9 0.0 copy-start.65
  35.0 0.1 collective-permute-start.5
  35.1 0.5 collective-permute-start.4
  35.6 0.7 fusion.129
  36.6 0.1 concatenate.133.small_ref
  36.8 34.0 %shard_map.203 = (bf16[256,1024]{1,0:T(8,128)(2,1)S(1)}, bf16[1024,256]{1,0:T(8,128)(2,1)S(1)}, f32[64,256]{1,0:T(8,128)S(1)}) custom-call(bf16[256,1024]{1,0:T(8,128)(2,1)S(1)} %convolution_convert_fusion.1.wide_ref, bf16[1024,256]{1,0:T(8,128)(2,1)S(1)} %convolution_convert_fusion.tall_ref, f32[64,256]{1,0:T(8,128)S(1)} %concatenate.133.small_ref), custom_call_target="tpu_custom_call" | custom-call | tf_op jit(solution)/shard_map/pallas_call | solution.py:203
  70.8 1.1 %convert_multiply_fusion.51 = f32[256,1024]{1,0:T(8,128)} fusion(bf16[256,1024]{1,0:T(8,128)(2,1)S(1)} %get-tuple-element.15), kind=kLoop, calls=%fused_computation.66 | loop fusion | flops 524288 | bytes 1572864 | tf_op jit(solution)/shard_map/mul | solution.py:399
  72.1 1.1 %convert_multiply_fusion.50 = f32[1024,256]{1,0:T(8,128)} fusion(bf16[1024,256]{1,0:T(8,128)(2,1)S(1)} %get-tuple-element.16), kind=kLoop, calls=%fused_computation.65 | loop fusion | flops 524288 | bytes 1572864 | tf_op jit(solution)/shard_map/mul | solution.py:401
  73.2 0.6 fusion.147
  73.8 0.0 collective-permute-done.5
  73.8 0.0 collective-permute-done.4
  73.8 0.1 pad_maximum_fusion.3
  73.9 1.3 %collective-permute-start.6 = (bf16[1,3,70,256]{3,2,1,0:T(8,128)(2,1)S(1)}, bf16[1,3,70,256]{3,2,1,0:T(8,128)(2,1)S(1)}, u32[]{:S(2)}, u32[]{:S(2)}) collective-permute-start(bf16[1,3,70,256]{3,2,1,0:T(8,128)(2,1)S(1)} %get-tuple-element.88), channel_id=1, source_target_pairs={{1,0},{2,1},{3,2},{4,3},{5,4},{6,5},{7,6},{8,7},{9,8},{10,9},{11,1... | collective-permute-start | bytes 322568 | tf_op jit(solution)/shard_map/ppermute | solution.py:235
  75.2 4.6 %collective-permute-start.7 = (bf16[1,3,70,256]{3,2,1,0:T(8,128)(2,1)S(1)}, bf16[1,3,70,256]{3,2,1,0:T(8,128)(2,1)S(1)}, u32[]{:S(2)}, u32[]{:S(2)}) collective-permute-start(bf16[1,3,70,256]{3,2,1,0:T(8,128)(2,1)S(1)} %get-tuple-element.89), channel_id=1, source_target_pairs={{0,1},{1,2},{2,3},{3,4},{4,5},{5,6},{6,7},{7,8},{8,9},{9,10},{10,1... | collective-permute-start | bytes 322568 | tf_op jit(solution)/shard_map/ppermute | solution.py:234
  79.8 0.6 copy.24
  80.4 0.6 reshape.295
  81.0 0.1 collective-permute-done.6
  81.1 1.7 %collective-permute-done.7 = bf16[1,3,70,256]{3,2,1,0:T(8,128)(2,1)S(1)} collective-permute-done((bf16[1,3,70,256]{3,2,1,0:T(8,128)(2,1)S(1)}, bf16[1,3,70,256]{3,2,1,0:T(8,128)(2,1)S(1)}, u32[]{:S(2)}, u32[]{:S(2)}) %collective-permute-start.7) | collective-permute-done | bytes 107552 | tf_op jit(solution)/shard_map/ppermute | solution.py:234
  82.8 0.1 pad_maximum_fusion.1
  83.2 3.8 %fusion.55 = bf16[1,6,64,256]{3,2,1,0:T(8,128)(2,1)} fusion(bf16[1,6,64,256]{3,2,1,0:T(8,128)(2,1)S(1)} %copy-done.2, bf16[1,6,64,256]{3,2,1,0:T(8,128)(2,1)S(1)} %bitcast.166, bf16[1,6,3,256]{3,2,1,0:T(4,128)(2,1)S(1)} %collective-permute-done.4, bf16[1,6,3,256]{3,2,1,0:T(4,128)(2,1)S(1)} %collective-permute-done.5, ...), kind=kLoop, calls=%fused_computation.167 | loop fusion | flops 16416768 | bytes 8915968 | tf_op jit(solution)/shard_map/convert_element_type | solution.py:368
  (153 shorter events, 0.6 us)
Async XLA Ops:
  0.6 23.2 %copy-start = (bf16[256,1024]{1,0:T(8,128)(2,1)S(1)}, bf16[256,1024]{1,0:T(8,128)(2,1)}, u32[]{:S(2)}) copy-start(bf16[256,1024]{1,0:T(8,128)(2,1)} %param.19) | copy-start | bytes 1572868
  0.7 19.0 %copy-start.1 = (bf16[1,6,64,256]{3,2,1,0:T(8,128)(2,1)S(1)}, bf16[1,6,64,256]{3,2,1,0:T(8,128)(2,1)}, u32[]{:S(2)}) copy-start(bf16[1,6,64,256]{3,2,1,0:T(8,128)(2,1)} %param.12) | copy-start | bytes 589828
  0.7 19.1 %copy-start.66 = (f32[256]{0:T(256)S(1)}, f32[256]{0:T(256)}, u32[]{:S(2)}) copy-start(f32[256]{0:T(256)} %param.16) | copy-start | bytes 3076
  1.5 5.4 %collective-permute-start = (bf16[1,6,3,256]{3,2,1,0:T(4,128)(2,1)S(1)}, bf16[1,6,3,256]{3,2,1,0:T(4,128)(2,1)S(1)}, u32[]{:S(2)}, u32[]{:S(2)}) collective-permute-start(bf16[1,6,3,256]{3,2,1,0:T(4,128)(2,1)S(1)} %get-tuple-element.98), channel_id=1, source_target_pairs={{0,16},{16,0},{1,17},{17,1},{2,18},{18,2},{3,19},{19,3},{4,20},{20... | collective-permute-start | bytes 27656 | tf_op jit(solution)/shard_map/ppermute | solution.py:234
  2.0 4.9 %collective-permute-start.1 = (bf16[1,6,3,256]{3,2,1,0:T(4,128)(2,1)S(1)}, bf16[1,6,3,256]{3,2,1,0:T(4,128)(2,1)S(1)}, u32[]{:S(2)}, u32[]{:S(2)}) collective-permute-start(bf16[1,6,3,256]{3,2,1,0:T(4,128)(2,1)S(1)} %get-tuple-element.99), channel_id=1, source_target_pairs={{16,0},{0,16},{17,1},{1,17},{18,2},{2,18},{19,3},{3,19},{20,4},{4,... | collective-permute-start | bytes 27656 | tf_op jit(solution)/shard_map/ppermute | solution.py:235
  4.0 18.9 %copy-start.3 = (f32[1,1,256]{2,1,0:T(1,128)}, f32[1,1,256]{2,1,0:T(1,128)S(1)}, u32[]{:S(2)}) copy-start(f32[1,1,256]{2,1,0:T(1,128)S(1)} %get-tuple-element.117) | copy-start | bytes 3076
  4.0 18.9 %copy-start.5 = (f32[1,1,256]{2,1,0:T(1,128)}, f32[1,1,256]{2,1,0:T(1,128)S(1)}, u32[]{:S(2)}) copy-start(f32[1,1,256]{2,1,0:T(1,128)S(1)} %get-tuple-element.118) | copy-start | bytes 3076
  4.0 18.9 %copy-start.7 = (f32[1,1,256]{2,1,0:T(1,128)}, f32[1,1,256]{2,1,0:T(1,128)S(1)}, u32[]{:S(2)}) copy-start(f32[1,1,256]{2,1,0:T(1,128)S(1)} %get-tuple-element.119) | copy-start | bytes 3076
  4.0 18.9 %copy-start.9 = (f32[1,1,256]{2,1,0:T(1,128)}, f32[1,1,256]{2,1,0:T(1,128)S(1)}, u32[]{:S(2)}) copy-start(f32[1,1,256]{2,1,0:T(1,128)S(1)} %get-tuple-element.120) | copy-start | bytes 3076
  4.1 18.9 %copy-start.11 = (f32[1,1,256]{2,1,0:T(1,128)}, f32[1,1,256]{2,1,0:T(1,128)S(1)}, u32[]{:S(2)}) copy-start(f32[1,1,256]{2,1,0:T(1,128)S(1)} %get-tuple-element.121) | copy-start | bytes 3076
  4.1 18.9 %copy-start.13 = (f32[1,1,256]{2,1,0:T(1,128)}, f32[1,1,256]{2,1,0:T(1,128)S(1)}, u32[]{:S(2)}) copy-start(f32[1,1,256]{2,1,0:T(1,128)S(1)} %get-tuple-element.122) | copy-start | bytes 3076
  4.1 18.9 %copy-start.15 = (f32[1,1,256]{2,1,0:T(1,128)}, f32[1,1,256]{2,1,0:T(1,128)S(1)}, u32[]{:S(2)}) copy-start(f32[1,1,256]{2,1,0:T(1,128)S(1)} %get-tuple-element.123) | copy-start | bytes 3076
  5.1 17.9 %copy-start.17 = (f32[1,1,256]{2,1,0:T(1,128)}, f32[1,1,256]{2,1,0:T(1,128)S(1)}, u32[]{:S(2)}) copy-start(f32[1,1,256]{2,1,0:T(1,128)S(1)} %get-tuple-element.124) | copy-start | bytes 3076
  5.1 17.9 %copy-start.19 = (f32[1,1,256]{2,1,0:T(1,128)}, f32[1,1,256]{2,1,0:T(1,128)S(1)}, u32[]{:S(2)}) copy-start(f32[1,1,256]{2,1,0:T(1,128)S(1)} %get-tuple-element.125) | copy-start | bytes 3076
  5.1 17.9 %copy-start.21 = (f32[1,1,256]{2,1,0:T(1,128)}, f32[1,1,256]{2,1,0:T(1,128)S(1)}, u32[]{:S(2)}) copy-start(f32[1,1,256]{2,1,0:T(1,128)S(1)} %get-tuple-element.126) | copy-start | bytes 3076
  5.2 17.9 %copy-start.23 = (f32[1,1,256]{2,1,0:T(1,128)}, f32[1,1,256]{2,1,0:T(1,128)S(1)}, u32[]{:S(2)}) copy-start(f32[1,1,256]{2,1,0:T(1,128)S(1)} %get-tuple-element.127) | copy-start | bytes 3076
  5.2 17.9 %copy-start.25 = (f32[1,1,256]{2,1,0:T(1,128)}, f32[1,1,256]{2,1,0:T(1,128)S(1)}, u32[]{:S(2)}) copy-start(f32[1,1,256]{2,1,0:T(1,128)S(1)} %get-tuple-element.128) | copy-start | bytes 3076
  5.2 17.9 %copy-start.27 = (f32[1,1,256]{2,1,0:T(1,128)}, f32[1,1,256]{2,1,0:T(1,128)S(1)}, u32[]{:S(2)}) copy-start(f32[1,1,256]{2,1,0:T(1,128)S(1)} %get-tuple-element.129) | copy-start | bytes 3076
  5.2 17.9 %copy-start.29 = (f32[1,1,256]{2,1,0:T(1,128)}, f32[1,1,256]{2,1,0:T(1,128)S(1)}, u32[]{:S(2)}) copy-start(f32[1,1,256]{2,1,0:T(1,128)S(1)} %get-tuple-element.130) | copy-start | bytes 3076
  5.2 17.9 %copy-start.31 = (f32[1,1,256]{2,1,0:T(1,128)}, f32[1,1,256]{2,1,0:T(1,128)S(1)}, u32[]{:S(2)}) copy-start(f32[1,1,256]{2,1,0:T(1,128)S(1)} %get-tuple-element.131) | copy-start | bytes 3076
  5.2 17.9 %copy-start.33 = (f32[1,1,256]{2,1,0:T(1,128)}, f32[1,1,256]{2,1,0:T(1,128)S(1)}, u32[]{:S(2)}) copy-start(f32[1,1,256]{2,1,0:T(1,128)S(1)} %get-tuple-element.132) | copy-start | bytes 3076
  5.2 17.9 %copy-start.35 = (f32[1,1,256]{2,1,0:T(1,128)}, f32[1,1,256]{2,1,0:T(1,128)S(1)}, u32[]{:S(2)}) copy-start(f32[1,1,256]{2,1,0:T(1,128)S(1)} %get-tuple-element.133) | copy-start | bytes 3076
  5.2 17.9 %copy-start.37 = (f32[1,1,256]{2,1,0:T(1,128)}, f32[1,1,256]{2,1,0:T(1,128)S(1)}, u32[]{:S(2)}) copy-start(f32[1,1,256]{2,1,0:T(1,128)S(1)} %get-tuple-element.134) | copy-start | bytes 3076
  5.2 17.9 %copy-start.39 = (f32[1,1,256]{2,1,0:T(1,128)}, f32[1,1,256]{2,1,0:T(1,128)S(1)}, u32[]{:S(2)}) copy-start(f32[1,1,256]{2,1,0:T(1,128)S(1)} %get-tuple-element.135) | copy-start | bytes 3076
  5.2 17.9 %copy-start.41 = (f32[1,1,256]{2,1,0:T(1,128)}, f32[1,1,256]{2,1,0:T(1,128)S(1)}, u32[]{:S(2)}) copy-start(f32[1,1,256]{2,1,0:T(1,128)S(1)} %get-tuple-element.136) | copy-start | bytes 3076
  5.3 17.9 %copy-start.43 = (f32[1,1,256]{2,1,0:T(1,128)}, f32[1,1,256]{2,1,0:T(1,128)S(1)}, u32[]{:S(2)}) copy-start(f32[1,1,256]{2,1,0:T(1,128)S(1)} %get-tuple-element.137) | copy-start | bytes 3076
  5.3 17.9 %copy-start.45 = (f32[1,1,256]{2,1,0:T(1,128)}, f32[1,1,256]{2,1,0:T(1,128)S(1)}, u32[]{:S(2)}) copy-start(f32[1,1,256]{2,1,0:T(1,128)S(1)} %get-tuple-element.138) | copy-start | bytes 3076
  5.3 17.9 %copy-start.47 = (f32[1,1,256]{2,1,0:T(1,128)}, f32[1,1,256]{2,1,0:T(1,128)S(1)}, u32[]{:S(2)}) copy-start(f32[1,1,256]{2,1,0:T(1,128)S(1)} %get-tuple-element.139) | copy-start | bytes 3076
  5.3 17.9 %copy-start.49 = (f32[1,1,256]{2,1,0:T(1,128)}, f32[1,1,256]{2,1,0:T(1,128)S(1)}, u32[]{:S(2)}) copy-start(f32[1,1,256]{2,1,0:T(1,128)S(1)} %get-tuple-element.140) | copy-start | bytes 3076
  5.3 17.9 %copy-start.51 = (f32[1,1,256]{2,1,0:T(1,128)}, f32[1,1,256]{2,1,0:T(1,128)S(1)}, u32[]{:S(2)}) copy-start(f32[1,1,256]{2,1,0:T(1,128)S(1)} %get-tuple-element.141) | copy-start | bytes 3076
  5.3 17.9 %copy-start.53 = (f32[1,1,256]{2,1,0:T(1,128)}, f32[1,1,256]{2,1,0:T(1,128)S(1)}, u32[]{:S(2)}) copy-start(f32[1,1,256]{2,1,0:T(1,128)S(1)} %get-tuple-element.142) | copy-start | bytes 3076
  8.0 7.4 %collective-permute-start.2 = (bf16[1,3,70,256]{3,2,1,0:T(8,128)(2,1)S(1)}, bf16[1,3,70,256]{3,2,1,0:T(8,128)(2,1)S(1)}, u32[]{:S(2)}, u32[]{:S(2)}) collective-permute-start(bf16[1,3,70,256]{3,2,1,0:T(8,128)(2,1)S(1)} %get-tuple-element.92), channel_id=1, source_target_pairs={{0,1},{1,2},{2,3},{3,4},{4,5},{5,6},{6,7},{7,8},{8,9},{9,10},{10,1... | collective-permute-start | bytes 322568 | tf_op jit(solution)/shard_map/ppermute | solution.py:234
  12.8 6.9 %collective-permute-start.3 = (bf16[1,3,70,256]{3,2,1,0:T(8,128)(2,1)S(1)}, bf16[1,3,70,256]{3,2,1,0:T(8,128)(2,1)S(1)}, u32[]{:S(2)}, u32[]{:S(2)}) collective-permute-start(bf16[1,3,70,256]{3,2,1,0:T(8,128)(2,1)S(1)} %get-tuple-element.93), channel_id=1, source_target_pairs={{1,0},{2,1},{3,2},{4,3},{5,4},{6,5},{7,6},{8,7},{9,8},{10,9},{11,1... | collective-permute-start | bytes 322568 | tf_op jit(solution)/shard_map/ppermute | solution.py:235
  19.8 4.0 %copy-start.55 = (f32[1024]{0:T(1024)S(1)}, f32[1024]{0:T(1024)}, u32[]{:S(2)}) copy-start(f32[1024]{0:T(1024)} %param.20) | copy-start | bytes 12292
  35.0 38.8 %collective-permute-start.5 = (bf16[1,6,3,256]{3,2,1,0:T(4,128)(2,1)S(1)}, bf16[1,6,3,256]{3,2,1,0:T(4,128)(2,1)S(1)}, u32[]{:S(2)}, u32[]{:S(2)}) collective-permute-start(bf16[1,6,3,256]{3,2,1,0:T(4,128)(2,1)S(1)} %get-tuple-element.96), channel_id=1, source_target_pairs={{16,0},{0,16},{17,1},{1,17},{18,2},{2,18},{19,3},{3,19},{20,4},{4,... | collective-permute-start | bytes 27656 | tf_op jit(solution)/shard_map/ppermute | solution.py:235
  35.1 38.7 %collective-permute-start.4 = (bf16[1,6,3,256]{3,2,1,0:T(4,128)(2,1)S(1)}, bf16[1,6,3,256]{3,2,1,0:T(4,128)(2,1)S(1)}, u32[]{:S(2)}, u32[]{:S(2)}) collective-permute-start(bf16[1,6,3,256]{3,2,1,0:T(4,128)(2,1)S(1)} %get-tuple-element.97), channel_id=1, source_target_pairs={{0,16},{16,0},{1,17},{17,1},{2,18},{18,2},{3,19},{19,3},{4,20},{20... | collective-permute-start | bytes 27656 | tf_op jit(solution)/shard_map/ppermute | solution.py:234
  71.9 11.0 %copy-start.4 = (f32[1,1,256]{2,1,0:T(1,128)S(1)}, f32[1,1,256]{2,1,0:T(1,128)}, u32[]{:S(2)}) copy-start(f32[1,1,256]{2,1,0:T(1,128)} %copy-done.3) | copy-start | bytes 3076
  71.9 11.0 %copy-start.6 = (f32[1,1,256]{2,1,0:T(1,128)S(1)}, f32[1,1,256]{2,1,0:T(1,128)}, u32[]{:S(2)}) copy-start(f32[1,1,256]{2,1,0:T(1,128)} %copy-done.5) | copy-start | bytes 3076
  71.9 11.0 %copy-start.8 = (f32[1,1,256]{2,1,0:T(1,128)S(1)}, f32[1,1,256]{2,1,0:T(1,128)}, u32[]{:S(2)}) copy-start(f32[1,1,256]{2,1,0:T(1,128)} %copy-done.7) | copy-start | bytes 3076
  71.9 11.0 %copy-start.10 = (f32[1,1,256]{2,1,0:T(1,128)S(1)}, f32[1,1,256]{2,1,0:T(1,128)}, u32[]{:S(2)}) copy-start(f32[1,1,256]{2,1,0:T(1,128)} %copy-done.9) | copy-start | bytes 3076
  71.9 11.0 %copy-start.12 = (f32[1,1,256]{2,1,0:T(1,128)S(1)}, f32[1,1,256]{2,1,0:T(1,128)}, u32[]{:S(2)}) copy-start(f32[1,1,256]{2,1,0:T(1,128)} %copy-done.11) | copy-start | bytes 3076
  71.9 11.0 %copy-start.14 = (f32[1,1,256]{2,1,0:T(1,128)S(1)}, f32[1,1,256]{2,1,0:T(1,128)}, u32[]{:S(2)}) copy-start(f32[1,1,256]{2,1,0:T(1,128)} %copy-done.13) | copy-start | bytes 3076
  71.9 11.0 %copy-start.16 = (f32[1,1,256]{2,1,0:T(1,128)S(1)}, f32[1,1,256]{2,1,0:T(1,128)}, u32[]{:S(2)}) copy-start(f32[1,1,256]{2,1,0:T(1,128)} %copy-done.15) | copy-start | bytes 3076
  72.0 11.0 %copy-start.18 = (f32[1,1,256]{2,1,0:T(1,128)S(1)}, f32[1,1,256]{2,1,0:T(1,128)}, u32[]{:S(2)}) copy-start(f32[1,1,256]{2,1,0:T(1,128)} %copy-done.17) | copy-start | bytes 3076
  72.0 11.0 %copy-start.20 = (f32[1,1,256]{2,1,0:T(1,128)S(1)}, f32[1,1,256]{2,1,0:T(1,128)}, u32[]{:S(2)}) copy-start(f32[1,1,256]{2,1,0:T(1,128)} %copy-done.19) | copy-start | bytes 3076
  72.0 11.0 %copy-start.22 = (f32[1,1,256]{2,1,0:T(1,128)S(1)}, f32[1,1,256]{2,1,0:T(1,128)}, u32[]{:S(2)}) copy-start(f32[1,1,256]{2,1,0:T(1,128)} %copy-done.21) | copy-start | bytes 3076
  72.0 11.0 %copy-start.24 = (f32[1,1,256]{2,1,0:T(1,128)S(1)}, f32[1,1,256]{2,1,0:T(1,128)}, u32[]{:S(2)}) copy-start(f32[1,1,256]{2,1,0:T(1,128)} %copy-done.23) | copy-start | bytes 3076
  72.0 11.0 %copy-start.26 = (f32[1,1,256]{2,1,0:T(1,128)S(1)}, f32[1,1,256]{2,1,0:T(1,128)}, u32[]{:S(2)}) copy-start(f32[1,1,256]{2,1,0:T(1,128)} %copy-done.25) | copy-start | bytes 3076
  72.0 11.0 %copy-start.28 = (f32[1,1,256]{2,1,0:T(1,128)S(1)}, f32[1,1,256]{2,1,0:T(1,128)}, u32[]{:S(2)}) copy-start(f32[1,1,256]{2,1,0:T(1,128)} %copy-done.27) | copy-start | bytes 3076
  72.0 11.0 %copy-start.30 = (f32[1,1,256]{2,1,0:T(1,128)S(1)}, f32[1,1,256]{2,1,0:T(1,128)}, u32[]{:S(2)}) copy-start(f32[1,1,256]{2,1,0:T(1,128)} %copy-done.29) | copy-start | bytes 3076
  72.0 11.0 %copy-start.32 = (f32[1,1,256]{2,1,0:T(1,128)S(1)}, f32[1,1,256]{2,1,0:T(1,128)}, u32[]{:S(2)}) copy-start(f32[1,1,256]{2,1,0:T(1,128)} %copy-done.31) | copy-start | bytes 3076
  72.0 11.0 %copy-start.34 = (f32[1,1,256]{2,1,0:T(1,128)S(1)}, f32[1,1,256]{2,1,0:T(1,128)}, u32[]{:S(2)}) copy-start(f32[1,1,256]{2,1,0:T(1,128)} %copy-done.33) | copy-start | bytes 3076
  72.0 11.0 %copy-start.36 = (f32[1,1,256]{2,1,0:T(1,128)S(1)}, f32[1,1,256]{2,1,0:T(1,128)}, u32[]{:S(2)}) copy-start(f32[1,1,256]{2,1,0:T(1,128)} %copy-done.35) | copy-start | bytes 3076
  72.1 11.0 %copy-start.38 = (f32[1,1,256]{2,1,0:T(1,128)S(1)}, f32[1,1,256]{2,1,0:T(1,128)}, u32[]{:S(2)}) copy-start(f32[1,1,256]{2,1,0:T(1,128)} %copy-done.37) | copy-start | bytes 3076
  72.1 11.0 %copy-start.40 = (f32[1,1,256]{2,1,0:T(1,128)S(1)}, f32[1,1,256]{2,1,0:T(1,128)}, u32[]{:S(2)}) copy-start(f32[1,1,256]{2,1,0:T(1,128)} %copy-done.39) | copy-start | bytes 3076
  72.1 11.0 %copy-start.42 = (f32[1,1,256]{2,1,0:T(1,128)S(1)}, f32[1,1,256]{2,1,0:T(1,128)}, u32[]{:S(2)}) copy-start(f32[1,1,256]{2,1,0:T(1,128)} %copy-done.41) | copy-start | bytes 3076
  72.1 11.0 %copy-start.44 = (f32[1,1,256]{2,1,0:T(1,128)S(1)}, f32[1,1,256]{2,1,0:T(1,128)}, u32[]{:S(2)}) copy-start(f32[1,1,256]{2,1,0:T(1,128)} %copy-done.43) | copy-start | bytes 3076
  72.1 11.0 %copy-start.46 = (f32[1,1,256]{2,1,0:T(1,128)S(1)}, f32[1,1,256]{2,1,0:T(1,128)}, u32[]{:S(2)}) copy-start(f32[1,1,256]{2,1,0:T(1,128)} %copy-done.45) | copy-start | bytes 3076
  72.1 11.0 %copy-start.48 = (f32[1,1,256]{2,1,0:T(1,128)S(1)}, f32[1,1,256]{2,1,0:T(1,128)}, u32[]{:S(2)}) copy-start(f32[1,1,256]{2,1,0:T(1,128)} %copy-done.47) | copy-start | bytes 3076
  72.1 11.0 %copy-start.50 = (f32[1,1,256]{2,1,0:T(1,128)S(1)}, f32[1,1,256]{2,1,0:T(1,128)}, u32[]{:S(2)}) copy-start(f32[1,1,256]{2,1,0:T(1,128)} %copy-done.49) | copy-start | bytes 3076
  72.1 11.0 %copy-start.52 = (f32[1,1,256]{2,1,0:T(1,128)S(1)}, f32[1,1,256]{2,1,0:T(1,128)}, u32[]{:S(2)}) copy-start(f32[1,1,256]{2,1,0:T(1,128)} %copy-done.51) | copy-start | bytes 3076
  72.1 11.0 %copy-start.54 = (f32[1,1,256]{2,1,0:T(1,128)S(1)}, f32[1,1,256]{2,1,0:T(1,128)}, u32[]{:S(2)}) copy-start(f32[1,1,256]{2,1,0:T(1,128)} %copy-done.53) | copy-start | bytes 3076
  73.9 7.2 %collective-permute-start.6 = (bf16[1,3,70,256]{3,2,1,0:T(8,128)(2,1)S(1)}, bf16[1,3,70,256]{3,2,1,0:T(8,128)(2,1)S(1)}, u32[]{:S(2)}, u32[]{:S(2)}) collective-permute-start(bf16[1,3,70,256]{3,2,1,0:T(8,128)(2,1)S(1)} %get-tuple-element.88), channel_id=1, source_target_pairs={{1,0},{2,1},{3,2},{4,3},{5,4},{6,5},{7,6},{8,7},{9,8},{10,9},{11,1... | collective-permute-start | bytes 322568 | tf_op jit(solution)/shard_map/ppermute | solution.py:235
  75.2 7.6 %collective-permute-start.7 = (bf16[1,3,70,256]{3,2,1,0:T(8,128)(2,1)S(1)}, bf16[1,3,70,256]{3,2,1,0:T(8,128)(2,1)S(1)}, u32[]{:S(2)}, u32[]{:S(2)}) collective-permute-start(bf16[1,3,70,256]{3,2,1,0:T(8,128)(2,1)S(1)} %get-tuple-element.89), channel_id=1, source_target_pairs={{0,1},{1,2},{2,3},{3,4},{4,5},{5,6},{6,7},{7,8},{8,9},{9,10},{10,1... | collective-permute-start | bytes 322568 | tf_op jit(solution)/shard_map/ppermute | solution.py:234
  (13 other events, 24.8 us)

commit v2 on v1

--- a/solution.py
+++ b/solution.py
@@ -145,48 +145,269 @@
             device, _ = partner(axis, stride, count, k)
             pl.semaphore_signal(barrier, inc=1, device_id=device, device_id_type=MESH)
             total += 1
-    pl.semaphore_wait(barrier, total)
-
-
-def sum_kernel(phases, steps, small_steps, wide_ref, tall_ref, small_ref, wide_out, tall_out, small_out, *scratch):
+    return total
+
+
+SIDES = [(dy, dx) for dy in (-1, 0, 1) for dx in (-1, 0, 1) if (dy, dx) != (0, 0)]
+EDGE = 16
+
+
+def on_grid(dy):
+    there = lax.axis_index("lat") + dy
+    return (there >= 0) & (there < lax.axis_size("lat"))
+
+
+def neighbour(dy, dx):
+    num_lon = lax.axis_size("lon")
+    return {
+        "lat": lax.axis_index("lat") + dy,
+        "lon": lax.rem(lax.axis_index("lon") + dx + num_lon, num_lon),
+    }
+
+
+def greet_neighbours(others):
+    barrier = pltpu.get_barrier_semaphore()
+    for dy in (-1, 0, 1):
+
+        @pl.when(on_grid(dy))
+        def _():
+            sides = [s for s in SIDES if s[0] == dy]
+            for side in sides:
+                pl.semaphore_signal(
+                    barrier, inc=1, device_id=neighbour(*side), device_id_type=MESH
+                )
+
+    lat, num_lat = lax.axis_index("lat"), lax.axis_size("lat")
+    around = jnp.minimum(lat, 1) + jnp.minimum(num_lat - 1 - lat, 1)
+    pl.semaphore_wait(barrier, others + 2 + 3 * around)
+
+
+class Halo:
+    def __init__(self, block, lands, send_sem, recv_sem):
+        self.block, self.lands = block, dict(zip(SIDES, lands))
+        self.send_sem, self.recv_sem = send_sem, recv_sem
+
+    def copy(self, side):
+        dy, dx = side
+        rows, cols, _ = self.block.shape
+        row = {1: pl.ds(rows - 3, 3), 0: pl.ds(0, rows), -1: pl.ds(0, 3)}[dy]
+        col = {1: pl.ds(cols - EDGE, EDGE), 0: pl.ds(0, cols), -1: pl.ds(0, EDGE)}[dx]
+        number = SIDES.index(side)
+        return pltpu.make_async_remote_copy(
+            src_ref=self.block.at[row, col],
+            dst_ref=self.lands[side],
+            send_sem=self.send_sem.at[number],
+            recv_sem=self.recv_sem.at[number],
+            device_id=neighbour(dy, dx),
+            device_id_type=MESH,
+        )
+
+    def each(self, sign, act):
+        for dy in (-1, 0, 1):
+
+            @pl.when(on_grid(sign * dy))
+            def _():
+                for side in SIDES:
+                    if side[0] == dy:
+                        act(self.copy(side))
+
+    def start(self):
+        self.each(1, lambda copy: copy.start())
+
+    def finish(self, pad):
+        self.each(-1, lambda copy: copy.wait_recv())
+        self.each(1, lambda copy: copy.wait_send())
+        rows, cols, channels = self.block.shape
+        for dy, first, count in ((1, 0, 3), (0, 3, rows), (-1, rows + 3, 3)):
+
+            @pl.when(on_grid(-dy))
+            def _():
+                middle = self.block if dy == 0 else self.lands[dy, 0]
+                here = pl.ds(first, count)
+                pad[here, 8 : 8 + cols] = middle[...].astype(jnp.float32)
+                left = self.lands[dy, 1][...].astype(jnp.float32)
+                right = self.lands[dy, -1][...].astype(jnp.float32)
+                pad[here, 0:8] = left[:, EDGE - 8 :]
+                pad[here, 8 + cols : 16 + cols] = right[:, :8]
+
+            if dy != 0:
+
+                @pl.when(jnp.logical_not(on_grid(-dy)))
+                def _():
+                    pad[pl.ds(first, count)] = jnp.zeros((count, cols + 16, channels), jnp.float32)
+
+
+def halo_scratch(rows, cols, channels):
+    lands = [
+        pltpu.VMEM((3 if dy else rows, EDGE if dx else cols, channels), jnp.bfloat16)
+        for dy, dx in SIDES
+    ]
+    return lands + [pltpu.SemaphoreType.DMA((8,))] * 2
+
+
+def convolve(pad, taps, begin, first, last, flip, store):
+    cols, channels = pad.shape[1] - 16, pad.shape[2]
+
+    def row_step(p, carry):
+        for h in range(channels // 128):
+            lanes = slice(h * 128, (h + 1) * 128)
+            total = begin(p, lanes)
+            for i in range(7):
+                for j in range(7):
+                    t = i * 7 + j
+                    t = 48 - t if flip else t
+                    total = total + pad[p + i, 5 + j : 5 + j + cols, lanes] * taps[t : t + 1, lanes]
+            store(p, lanes, total)
+        return carry
+
+    lax.fori_loop(first, last, row_step, 0)
+
+
+def correlate(pad, grad, out):
+    rows, cols, channels = grad.shape
+    for h in range(channels // 128):
+        lanes = slice(h * 128, (h + 1) * 128)
+        for j in range(7):
+
+            def row_step(p, sums):
+                own = grad[p, :, lanes].astype(jnp.float32)
+                new = []
+                for i in range(7):
+                    term = pad[p + i, 5 + j : 5 + j + cols, lanes] * own
+                    new.append(sums[i] + jnp.sum(term.reshape(cols // 8, 8, 128), axis=0))
+                return tuple(new)
+
+            sums = lax.fori_loop(
+                0, rows, row_step, tuple(jnp.zeros((8, 128), jnp.float32) for _ in range(7))
+            )
+            for i in range(7):
+                out[i * 7 + j : i * 7 + j + 1, lanes] = jnp.sum(sums[i], axis=0, keepdims=True)
+
+
+def depth_kernel(state, taps, bias, depth_out, pad, *scratch):
+    halo = Halo(state, scratch[:8], *scratch[8:])
+    greet_neighbours(0)
+    halo.start()
+    halo.finish(pad)
+    cols = state.shape[1]
+
+    def begin(p, lanes):
+        return jnp.broadcast_to(bias[:, lanes], (cols, 128))
+
+    def store(p, lanes, total):
+        depth_out[p, :, lanes] = total
+
+    convolve(pad, taps, begin, 0, state.shape[0], False, store)
+
+
+def depth_of(state, taps, bias):
+    rows, cols, channels = state.shape
+    vmem = pl.BlockSpec(memory_space=pltpu.VMEM)
+    return pl.pallas_call(
+        depth_kernel,
+        out_shape=(
+            jax.ShapeDtypeStruct(state.shape, jnp.float32),
+            jax.ShapeDtypeStruct((rows + 6, cols + 16, channels), jnp.float32),
+        ),
+        in_specs=[vmem] * 3,
+        out_specs=(vmem,) * 2,
+        scratch_shapes=halo_scratch(rows, cols, channels),
+        compiler_params=pltpu.CompilerParams(
+            collective_id=1, has_side_effects=True, vmem_limit_bytes=40 * 1024 * 1024
+        ),
+    )(state, taps, bias[None])
+
+
+def final_kernel(phases, steps, small_steps, wide_ref, tall_ref, other_ref, grad_ref, pad_ref, cot_ref,
+                 taps_ref, wide_out, tall_out, small_out, state_out, *scratch):
     num = len(phases)
-    mine, whole, small_whole = scratch[:3]
-    landing = scratch[3 : 3 + num]
-    small_landing = scratch[3 + num : 3 + 2 * num]
-    sems = scratch[3 + 2 * num :]
+    small_mine, mine, whole, small_whole, grad_pad = scratch[:5]
+    scratch = scratch[5:]
+    halo = Halo(grad_ref, scratch[:8], *scratch[8:10])
+    landing = scratch[10 : 10 + num]
+    small_landing = scratch[10 + num : 10 + 2 * num]
+    sems = scratch[10 + 2 * num :]
     channels = tall_ref.shape[1]
     depth = wide_ref.shape[0]
     tall = tall_ref.shape[0]
     blocks = wide_ref.shape[1] // channels
-    greet(phases)
+    rows = grad_ref.shape[0]
+    greet_neighbours(greet(phases))
+    halo.start()
     mine[0:tall] = tall_ref[...]
     for b in range(blocks):
         mine[tall + b * depth : tall + (b + 1) * depth] = wide_ref[:, b * channels : (b + 1) * channels]
     big = Reducer(16, steps, mine, whole, landing, *sems[:4])
-    small = Reducer(8, small_steps, small_ref, small_whole, small_landing, *sems[4:])
-    for number in range(num):
-        big.scatter_start(number)
-        small.scatter_start(number)
-        small.scatter_finish(number, number == num - 1)
-        big.scatter_finish(number, number == num - 1)
-    for number in reversed(range(num)):
-        big.gather_start(number)
-        small.gather_start(number)
-        small.gather_finish(number)
-        big.gather_finish(number)
+    small = Reducer(8, small_steps, small_mine, small_whole, small_landing, *sems[4:])
+
+    def small_terms():
+        used = 49 + other_ref.shape[0]
+        small_mine[49:used] = other_ref[...]
+        if used < small_mine.shape[0]:
+            small_mine[used:] = jnp.zeros((small_mine.shape[0] - used, channels), jnp.float32)
+        correlate(pad_ref, grad_ref, small_mine)
+
+    def begin(p, lanes):
+        return cot_ref[p, :, lanes].astype(jnp.float32)
+
+    def store(p, lanes, total):
+        state_out[p, :, lanes] = total.astype(jnp.bfloat16)
+
+    def near_rows():
+        halo.finish(grad_pad)
+        convolve(grad_pad, taps_ref, begin, 0, rows // 2, True, store)
+
+    def far_rows():
+        convolve(grad_pad, taps_ref, begin, rows // 2, rows, True, store)
+
+    def chain(reducer):
+        moves = []
+        for n in range(num):
+            moves.append(
+                (
+                    functools.partial(reducer.scatter_start, n),
+                    functools.partial(reducer.scatter_finish, n, n == num - 1),
+                )
+            )
+        for n in reversed(range(num)):
+            if reducer.steps[n][3]:
+                moves.append(
+                    (
+                        functools.partial(reducer.gather_start, n),
+                        functools.partial(reducer.gather_finish, n),
+                    )
+                )
+        return moves
+
+    lag = 2
+    big_moves, small_moves = chain(big), chain(small)
+    beside = {1: small_terms, 2: near_rows, 3: far_rows}
+    for t in range(max(len(big_moves), len(small_moves) + lag)):
+        moves = []
+        if 0 <= t - lag < len(small_moves):
+            moves.append(small_moves[t - lag])
+        if t < len(big_moves):
+            moves.append(big_moves[t])
+        for start, _ in reversed(moves):
+            start()
+        if t in beside:
+            beside[t]()
+        for _, finish in moves:
+            finish()
     small_out[...] = small_whole[...]
     tall_out[...] = whole[0:tall]
     for b in range(blocks):
         wide_out[:, b * channels : (b + 1) * channels] = whole[tall + b * depth : tall + (b + 1) * depth]
 
 
-def summed_over_devices(wide, tall, small):
+def final_of(wide, tall, other, grad, pad, cot, taps):
     phases = phases_of(lax.axis_size("lon"), lax.axis_size("lat"))
     num = len(phases)
     channels = tall.shape[1]
     rows = tall.shape[0] + wide.shape[1] // channels * wide.shape[0]
+    small_rows = -(-(49 + other.shape[0]) // 64) * 64
     steps, _ = plan(rows, 16, phases)
-    small_steps, _ = plan(small.shape[0], 8, phases)
+    small_steps, _ = plan(small_rows, 8, phases)
 
     def landings(which, dtype):
         return [
@@ -195,25 +416,24 @@
         ]
 
     vmem = pl.BlockSpec(memory_space=pltpu.VMEM)
-
-    def body(wide_ref, tall_ref, small_ref, wide_out, tall_out, small_out, small_mine, *scratch):
-        small_mine[...] = small_ref[...]
-        sum_kernel(phases, steps, small_steps, wide_ref, tall_ref, small_mine, wide_out, tall_out, small_out, *scratch)
-
+    small = (small_rows, channels)
     return pl.pallas_call(
-        body,
+        functools.partial(final_kernel, phases, steps, small_steps),
         out_shape=(
             jax.ShapeDtypeStruct(wide.shape, jnp.bfloat16),
             jax.ShapeDtypeStruct(tall.shape, jnp.bfloat16),
-            jax.ShapeDtypeStruct(small.shape, jnp.float32),
+            jax.ShapeDtypeStruct(small, jnp.float32),
+            jax.ShapeDtypeStruct(grad.shape, jnp.bfloat16),
         ),
-        in_specs=[vmem] * 3,
-        out_specs=(vmem,) * 3,
+        in_specs=[vmem] * 7,
+        out_specs=(vmem,) * 4,
         scratch_shapes=[
-            pltpu.VMEM(small.shape, jnp.float32),
+            pltpu.VMEM(small, jnp.float32),
             pltpu.VMEM((rows, channels), jnp.bfloat16),
             pltpu.VMEM((rows, channels), jnp.bfloat16),
-            pltpu.VMEM(small.shape, jnp.float32),
+            pltpu.VMEM(small, jnp.float32),
+            pltpu.VMEM(pad.shape, jnp.float32),
+            *halo_scratch(*grad.shape),
             *landings(steps, jnp.bfloat16),
             *landings(small_steps, jnp.float32),
             *[pltpu.SemaphoreType.DMA((num, 4))] * 8,
@@ -221,62 +441,7 @@
         compiler_params=pltpu.CompilerParams(
             collective_id=0, has_side_effects=True, vmem_limit_bytes=40 * 1024 * 1024
         ),
-    )(wide, tall, small)
-
-
-def extended(array, sides, width, wrap):
-    for axis, dim in sides:
-        size, length = (lax.axis_size(axis), array.shape[dim])
-        up = [(i, (i + 1) % size) for i in range(size if wrap else size - 1)]
-        down = [(j, i) for i, j in up]
-        last = lax.slice_in_dim(array, length - width, length, axis=dim)
-        leading = lax.slice_in_dim(array, 0, width, axis=dim)
-        before = lax.ppermute(last, axis, up)
-        after = lax.ppermute(leading, axis, down)
-        array = jnp.concatenate([before, array, after], axis=dim)
-    return array
-
-
-def depthwise(padded, kernel, num_rows, num_cols):
-    summed = jnp.zeros((padded.shape[0], num_rows, num_cols, padded.shape[3]), jnp.float32)
-    for row_off in range(7):
-        for col_off in range(7):
-            summed = (
-                summed
-                + padded[:, row_off : row_off + num_rows, col_off : col_off + num_cols, :].astype(
-                    jnp.float32
-                )
-                * kernel[row_off, col_off]
-            )
-    return summed
-
-
-def transposed(padded, kernel, num_rows, num_cols):
-    summed = jnp.zeros((padded.shape[0], num_rows, num_cols, padded.shape[3]), jnp.float32)
-    for row_off in range(7):
-        for col_off in range(7):
-            summed = (
-                summed
-                + padded[
-                    :, 6 - row_off : 6 - row_off + num_rows, 6 - col_off : 6 - col_off + num_cols, :
-                ].astype(jnp.float32)
-                * kernel[row_off, col_off]
-            )
-    return summed
-
-
-def kernel_terms(padded, grad_depth, num_rows, num_cols):
-    grad_float = grad_depth.astype(jnp.float32)
-    rows_out = []
-    for row_off in range(7):
-        cols_out = []
-        for col_off in range(7):
-            window = padded[
-                :, row_off : row_off + num_rows, col_off : col_off + num_cols, :
-            ].astype(jnp.float32)
-            cols_out.append(jnp.sum(window * grad_float, axis=(0, 1, 2)))
-        rows_out.append(jnp.stack(cols_out))
-    return jnp.stack(rows_out)
+    )(wide, tall, other, grad, pad, cot, taps)
 
 
 def forward_tokens(depth_out, ln_gain, ln_bias, w_in, b_in, w_out, b_out):
@@ -343,9 +508,8 @@
 ):
     num_batch, num_rows, num_cols, channels = ocean_state.shape
     mask_float = land_sea.astype(jnp.float32)[..., None]
-    lon_ext = extended(ocean_state, (("lon", 2),), 3, True)
-    padded = extended(lon_ext, (("lat", 1),), 3, False)
-    depth_out = depthwise(padded, dw_kernel, num_rows, num_cols) + dw_bias
+    taps = dw_kernel.reshape(-1, channels)
+    depth_out, padded = depth_of(ocean_state[0], taps, dw_bias)
     masked = (mask_float * cotangent.astype(jnp.float32)).reshape(-1, channels)
     norm_hat, inv_std, normed, pre_act, activated, branch = forward_tokens(
         depth_out.reshape(-1, channels), ln_gain, ln_bias, w_in, b_in, w_out, b_out
@@ -357,22 +521,15 @@
         masked, branch, grad_branch, activated, normed, grad_pre, grad_norm, norm_hat
     )
     grad_depth = grad_flat.reshape(num_batch, num_rows, num_cols, channels)
-    grad_ext = extended(grad_depth, (("lon", 2),), 3, True)
-    grad_pad = extended(grad_ext, (("lat", 1),), 3, False)
     branch_own = branch.reshape(num_batch, num_rows, num_cols, channels)
     output = (ocean_state.astype(jnp.float32) + mask_float * layer_scale * branch_own).astype(
         jnp.bfloat16
     )
-    grad_state = (
-        cotangent.astype(jnp.float32) + transposed(grad_pad, dw_kernel, num_rows, num_cols)
-    ).astype(jnp.bfloat16)
-    kernel_part = kernel_terms(padded, grad_depth, num_rows, num_cols)
     bias_part = jnp.sum(grad_depth.astype(jnp.float32), axis=(0, 1, 2))
     grad_w_in, grad_w_out, grad_b_in, grad_b_out, grad_scale, grad_ln_gain, grad_ln_bias = (
         grad_terms
     )
     rows = [
-        kernel_part.reshape(-1, channels),
         bias_part[None],
         grad_ln_gain[None],
         grad_ln_bias[None],
@@ -380,11 +537,16 @@
         grad_scale[None],
         grad_b_in.reshape(-1, channels),
     ]
-    used = sum(r.shape[0] for r in rows)
-    small = jnp.concatenate(rows + [jnp.zeros((-used % 64, channels), jnp.float32)])
-    grad_w_in, grad_w_out, small = summed_over_devices(
-        grad_w_in.astype(jnp.bfloat16), grad_w_out.astype(jnp.bfloat16), small
-    )
+    grad_w_in, grad_w_out, small, grad_state = final_of(
+        grad_w_in.astype(jnp.bfloat16),
+        grad_w_out.astype(jnp.bfloat16),
+        jnp.concatenate(rows),
+        grad_depth[0],
+        padded,
+        cotangent[0],
+        taps,
+    )
+    grad_state = grad_state[None]
     grad_w_in, grad_w_out = (grad_w_in.astype(jnp.float32), grad_w_out.astype(jnp.float32))
     all_cells = num_batch * num_rows * num_cols * lax.axis_size("lon") * lax.axis_size("lat")
     factor = 1.0 / jnp.sqrt(jnp.float32(all_cells))

time: 88.5 us -> 76.3 us (0.86); the launches traced: 86.9 us -> 75.9 us
  Pallas kernels: 34 us -> 52.5 us
  starting transfers between devices: 13.1 us -> 0 us
  other arithmetic: 16.6 us -> 6.47 us
  waiting for transfers between devices: 7.34 us -> 0 us
  matrix products: 6.16 us -> 8.24 us
  between operations: 1.9 us -> 0.88 us
    pallas_call x1 -> x2, Pallas kernels: 34 us -> 52.5 us  [the longest x1 39 us: final_of(): pl.pallas_call(functools.partial(final_kernel, phases, steps, small_steps...]
    ppermute x8 -> x0, starting transfers between devices: 13.1 us -> none  [the longest x4 10.4 us: extended(): before = lax.ppermute(last, axis, up)]
    ppermute x8 -> x0, waiting for transfers between devices: 7.34 us -> none  [the longest x4 4.42 us: extended(): after = lax.ppermute(leading, axis, down)]
    slice x7 -> x0, local copies, waits for them, and re-layouts: 3.8 us -> none  [the longest x3 2.92 us: depthwise(): kernel[row_off, col_off]]
    convert_element_type x1 -> x0, other arithmetic: 3.77 us -> none  [local(): grad_state = (cotangent.astype(jnp.float32) + transposed(grad_pad, dw_ker...]
    unnamed x148 -> x34, local copies, waits for them, and re-layouts: 2.22 us -> 5.5 us
    reduce_sum x1, other arithmetic: 3.15 us -> 0.12 us  [forward_tokens(): center = depth_out - jnp.mean(depth_out, axis=-1, keepdims=True)]
    reduce_sum x3 -> x0, other arithmetic: 2.27 us -> none  [kernel_terms(): cols_out.append(jnp.sum(window * grad_float, axis=(0, 1, 2)))]
  transfers between devices with their start and end apart: 8 -> 0, of which waited for: 4 -> 0; matrix products, arithmetic and copies ran while one was open for 11% -> 0% of each run, Pallas kernels for 39% -> 0%
where the time goes in v2:
time: 76.3 us; the launch traced here: 75.9 us
  Pallas kernels  52.5 us (69%)
  matrix products  8.24 us (11%)
  local copies, waits for them, and re-layouts  7.82 us (10%)
  other arithmetic  6.47 us (8%)
  between operations  0.88 us (1%)
    pallas_call x1, Pallas kernels, final_of(): pl.pallas_call(functools.partial(final_kernel, phases, steps, small_steps...  39 us
    pallas_call x1, Pallas kernels, depth_of(): pl.pallas_call(depth_kernel, out_shape=(jax.ShapeDtypeStruct(state.shape,...  13.5 us
    unnamed x34, local copies, waits for them, and re-layouts  5.5 us
    dot_general x1, matrix products, backward_tokens(): lax.dot_general(grad_branch, w_out, (((1,), (1,)), ((), ())), preferred_e...  2.17 us
    mul x1, other arithmetic, local(): grad_w_in * factor  2.17 us
    dot_general x1, matrix products, forward_tokens(): jnp.dot(activated, w_out, preferred_element_type=jnp.float32) + b_out  1.73 us
    dot_general x1, matrix products, backward_tokens(): lax.dot_general(grad_pre, w_in, (((1,), (1,)), ((), ())), preferred_eleme...  1.66 us
    dot_general x1, matrix products, weight_terms(): lax.dot_general(normed, grad_pre, dims, preferred_element_type=jnp.float32)  1.59 us

profile of v2, /device:TPU:0, one launch (start us, length us, event | category | flops | bytes accessed | tf_op | source)
XLA Modules:
  0.0 75.9 jit_solution(13657671804443068408)
XLA Ops:
  0.6 0.0 copy-start
  0.7 0.0 copy-start.10
  0.7 0.7 convert_element_type.56
  1.4 0.8 %reshape.118.taps.taps_ref = f32[49,256]{1,0:T(8,128)S(1)} reshape(f32[7,7,256]{2,1,0:T(8,128)} %param.15) | data formatting | bytes 100352 | tf_op jit(solution)/shard_map/reshape | solution.py:511
  2.2 0.0 copy-start.2
  2.3 0.9 %copy-done.2 = bf16[1,6,64,256]{3,2,1,0:T(8,128)(2,1)S(1)} copy-done((bf16[1,6,64,256]{3,2,1,0:T(8,128)(2,1)S(1)}, bf16[1,6,64,256]{3,2,1,0:T(8,128)(2,1)}, u32[]{:S(2)}) %copy-start.2) | copy-done | bytes 196632
  3.2 0.0 copy-start.9
  3.2 0.7 copy-done.9
  3.9 13.5 %shard_map.203 = (f32[6,64,256]{2,1,0:T(8,128)S(1)}, f32[12,80,256]{2,1,0:T(8,128)S(1)}) custom-call(bf16[6,64,256]{2,1,0:T(8,128)(2,1)S(1)} %bitcast.54, f32[49,256]{1,0:T(8,128)S(1)} %reshape.118.taps.taps_ref, f32[1,256]{1,0:T(1,128)S(1)} %bitcast.56), custom_call_target="tpu_custom_call" | custom-call | tf_op jit(solution)/shard_map/pallas_call | solution.py:306
  17.3 0.1 reduce_sum.90
  17.5 0.1 div.15
  17.5 0.0 copy-start.14
  17.5 0.2 multiply_reduce_fusion.2
  17.8 0.1 rsqrt.12
  17.9 0.9 %add_convert_fusion.1 = bf16[384,256]{1,0:T(8,128)(2,1)S(1)} fusion(f32[6,64,256]{2,1,0:T(8,128)S(1)} %get-tuple-element.17, f32[256]{0:T(256)} %param.18, f32[256]{0:T(256)} %param.17, f32[384]{0:T(512)S(1)} %rsqrt.12, f32[384]{0:T(512)S(1)} %div.15), kind=kLoop, calls=%fused_computation.31 | loop fusion | flops 491520 | bytes 594944 | tf_op jit(solution)/shard_map/convert_element_type | solution.py:451
  18.8 0.0 copy-done
  18.8 0.0 copy-done.10
  18.8 0.4 convolution_add_fusion
  19.2 0.0 copy-done.14
  19.2 0.0 copy-start.1
  19.2 0.0 copy-start.3
  19.2 0.0 copy-start.12
  19.2 1.7 %convolution_add_fusion.1 = f32[384,256]{1,0:T(8,128)S(1)} fusion(bf16[1024,256]{1,0:T(8,128)(2,1)} %param.21, f32[256]{0:T(256)S(1)} %copy-done.14, f32[384,1024]{1,0:T(8,128)S(1)} %convolution_add_fusion), kind=kOutput, calls=%fused_computation.14 | convolution fusion | flops 204963840 | bytes 2491392 | tf_op jit(solution)/shard_map/dot_general | solution.py:454
  20.9 0.0 copy-done.1
  20.9 0.0 copy-done.3
  21.0 0.0 copy-done.12
  21.0 0.9 %convert_reduce_fusion.1 = (f32[256]{0:T(256)S(1)}, f32[1,6,64,256]{3,2,1,0:T(8,128)S(1)}, bf16[1,6,64,256]{3,2,1,0:T(8,128)(2,1)}) fusion(f32[256]{0:T(256)S(1)} %copy-done.12, bf16[1,6,64,256]{3,2,1,0:T(8,128)(2,1)S(1)} %copy-done.1, f32[6,64]{1,0:T(8,128)S(1)} %bitcast.58, f32[1,6,64,256]{3,2,1,0:T(8,128)S(1)} %bitcast.57, ...), kind=kLoop, calls=%fused_computation.23 | loop fusion | flops 1081088 | bytes 1379840 | tf_op jit(solution)/shard_map/reduce_sum | solution.py:488
  21.8 0.1 fusion.8
  21.9 0.0 copy-start.13
  21.9 0.7 convolution_convert_fusion.tall_ref
  22.6 0.3 copy-done.13
  23.0 0.0 copy-start.11
  23.0 2.2 %convert_reduce_fusion = (f32[1024]{0:T(1024)S(1)}, bf16[384,1024]{1,0:T(8,128)(2,1)}) fusion(f32[384,1024]{1,0:T(8,128)S(1)} %convolution_add_fusion, bf16[384,256]{1,0:T(8,128)(2,1)S(1)} %get-tuple-element.30, bf16[1024,256]{1,0:T(8,128)(2,1)S(1)} %copy-done.13), kind=kOutput, calls=%fused_computation.9 | convolution fusion | flops 209976320 | bytes 3084288 | tf_op jit(solution)/shard_map/dot_general | solution.py:460
  25.1 1.6 %convolution_convert_fusion.1.wide_ref = bf16[256,1024]{1,0:T(8,128)(2,1)S(1)} fusion(bf16[384,256]{1,0:T(8,128)(2,1)S(1)} %add_convert_fusion.1, bf16[384,1024]{1,0:T(8,128)(2,1)} %get-tuple-element.41), kind=kOutput, calls=%fused_computation.13 | convolution fusion | flops 201588736 | bytes 1507328 | tf_op jit(solution)/shard_map/dot_general | solution.py:482
  26.7 0.0 copy-done.11
  26.7 1.7 %multiply_reduce_fusion = (f32[256]{0:T(256)S(1)}, f32[384]{0:T(512)S(1)}, f32[384]{0:T(512)S(1)}, f32[256]{0:T(256)S(1)}, f32[384,256]{1,0:T(8,128)S(1)}) fusion(f32[6,64,256]{2,1,0:T(8,128)S(1)} %get-tuple-element.17, f32[384]{0:T(512)S(1)} %rsqrt.12, f32[384]{0:T(512)S(1)} %div.15, f32[256]{0:T(256)S(1)} %copy-done.11, ...), kind=kOutput, calls=%fused_computation.25 | convolution fusion | flops 202210048 | bytes 2106368 | tf_op jit(solution)/shard_map/dot_general | solution.py:465
  28.4 0.3 convert_reduce_fusion.2
  28.7 0.1 concatenate.3.other_ref
  28.8 39.0 %shard_map.204 = (bf16[256,1024]{1,0:T(8,128)(2,1)S(1)}, bf16[1024,256]{1,0:T(8,128)(2,1)S(1)}, f32[64,256]{1,0:T(8,128)S(1)}, bf16[6,64,256]{2,1,0:T(8,128)(2,1)S(1)}) custom-call(bf16[256,1024]{1,0:T(8,128)(2,1)S(1)} %convolution_convert_fusion.1.wide_ref, bf16[1024,256]{1,0:T(8,128)(2,1)S(1)} %convolution_convert_fusion.tall_ref, ...), custom_call_target="tpu_custom_call" | custom-call | tf_op jit(solution)/shard_map/pallas_call | solution.py:420
  67.9 0.0 copy-start.4
  67.9 0.8 %copy-done.4 = bf16[1024,256]{1,0:T(8,128)(2,1)} copy-done((bf16[1024,256]{1,0:T(8,128)(2,1)}, bf16[1024,256]{1,0:T(8,128)(2,1)S(1)}, u32[]{:S(2)}) %copy-start.4) | copy-done | bytes 524312
  68.7 0.0 copy-start.6
  68.7 0.8 %copy-done.6 = bf16[256,1024]{1,0:T(8,128)(2,1)} copy-done((bf16[256,1024]{1,0:T(8,128)(2,1)}, bf16[256,1024]{1,0:T(8,128)(2,1)S(1)}, u32[]{:S(2)}) %copy-start.6) | copy-done | bytes 524312
  69.5 0.0 copy-start.7
  69.5 0.7 copy-done.7
  70.2 0.0 copy-start.5
  70.2 0.6 copy.24
  70.8 0.6 fusion.10
  71.4 0.6 reshape.123
  72.0 0.0 copy-start.8
  72.0 2.2 %convert_multiply_fusion.1 = f32[256,1024]{1,0:T(8,128)} fusion(bf16[256,1024]{1,0:T(8,128)(2,1)} %copy-done.6), kind=kLoop, calls=%fused_computation.16 | loop fusion | flops 524288 | bytes 1572864 | tf_op jit(solution)/shard_map/mul | solution.py:561
  74.2 0.0 copy-done.5
  74.2 1.1 %convert_multiply_fusion = f32[1024,256]{1,0:T(8,128)} fusion(bf16[1024,256]{1,0:T(8,128)(2,1)S(1)} %copy-done.5), kind=kLoop, calls=%fused_computation.15 | loop fusion | flops 524288 | bytes 1572864 | tf_op jit(solution)/shard_map/mul | solution.py:563
  75.2 0.0 copy-done.8
  75.2 0.7 copy.28
  (8 shorter events, 0.0 us)
Async XLA Ops:
  0.6 18.1 %copy-start = (bf16[256,1024]{1,0:T(8,128)(2,1)S(1)}, bf16[256,1024]{1,0:T(8,128)(2,1)}, u32[]{:S(2)}) copy-start(bf16[256,1024]{1,0:T(8,128)(2,1)} %param.19) | copy-start | bytes 1572868
  0.7 18.1 %copy-start.10 = (f32[1024]{0:T(1024)S(1)}, f32[1024]{0:T(1024)}, u32[]{:S(2)}) copy-start(f32[1024]{0:T(1024)} %param.20) | copy-start | bytes 12292
  2.2 0.9 %copy-start.2 = (bf16[1,6,64,256]{3,2,1,0:T(8,128)(2,1)S(1)}, bf16[1,6,64,256]{3,2,1,0:T(8,128)(2,1)}, u32[]{:S(2)}) copy-start(bf16[1,6,64,256]{3,2,1,0:T(8,128)(2,1)} %param.12) | copy-start | bytes 589828
  3.2 0.7 copy-start.9
  17.5 1.6 %copy-start.14 = (f32[256]{0:T(256)S(1)}, f32[256]{0:T(256)}, u32[]{:S(2)}) copy-start(f32[256]{0:T(256)} %param.22) | copy-start | bytes 3076
  19.2 1.8 %copy-start.1 = (bf16[1,6,64,256]{3,2,1,0:T(8,128)(2,1)S(1)}, bf16[1,6,64,256]{3,2,1,0:T(8,128)(2,1)}, u32[]{:S(2)}) copy-start(bf16[1,6,64,256]{3,2,1,0:T(8,128)(2,1)} %param.14) | copy-start | bytes 589828
  19.2 1.8 %copy-start.3 = (bf16[1,6,64,256]{3,2,1,0:T(8,128)(2,1)S(1)}, bf16[1,6,64,256]{3,2,1,0:T(8,128)(2,1)}, u32[]{:S(2)}) copy-start(bf16[1,6,64,256]{3,2,1,0:T(8,128)(2,1)} %param.12) | copy-start | bytes 589828
  19.2 1.8 %copy-start.12 = (f32[256]{0:T(256)S(1)}, f32[256]{0:T(256)}, u32[]{:S(2)}) copy-start(f32[256]{0:T(256)} %param.23) | copy-start | bytes 3076
  21.9 1.0 %copy-start.13 = (bf16[1024,256]{1,0:T(8,128)(2,1)S(1)}, bf16[1024,256]{1,0:T(8,128)(2,1)}, u32[]{:S(2)}) copy-start(bf16[1024,256]{1,0:T(8,128)(2,1)} %param.21) | copy-start | bytes 1572868
  23.0 3.8 %copy-start.11 = (f32[256]{0:T(256)S(1)}, f32[256]{0:T(256)}, u32[]{:S(2)}) copy-start(f32[256]{0:T(256)} %param.17) | copy-start | bytes 3076
  67.9 0.8 %copy-start.4 = (bf16[1024,256]{1,0:T(8,128)(2,1)}, bf16[1024,256]{1,0:T(8,128)(2,1)S(1)}, u32[]{:S(2)}) copy-start(bf16[1024,256]{1,0:T(8,128)(2,1)S(1)} %get-tuple-element.22) | copy-start | bytes 1572868
  68.7 0.8 %copy-start.6 = (bf16[256,1024]{1,0:T(8,128)(2,1)}, bf16[256,1024]{1,0:T(8,128)(2,1)S(1)}, u32[]{:S(2)}) copy-start(bf16[256,1024]{1,0:T(8,128)(2,1)S(1)} %get-tuple-element.21) | copy-start | bytes 1572868
  69.5 0.7 copy-start.7
  70.2 4.0 %copy-start.5 = (bf16[1024,256]{1,0:T(8,128)(2,1)S(1)}, bf16[1024,256]{1,0:T(8,128)(2,1)}, u32[]{:S(2)}) copy-start(bf16[1024,256]{1,0:T(8,128)(2,1)} %copy-done.4) | copy-start | bytes 1572868
  72.0 3.2 %copy-start.8 = (bf16[6,64,256]{2,1,0:T(8,128)(2,1)S(1)}, bf16[6,64,256]{2,1,0:T(8,128)(2,1)}, u32[]{:S(2)}) copy-start(bf16[6,64,256]{2,1,0:T(8,128)(2,1)} %copy-done.7) | copy-start | bytes 589828

commit v3 on v2

--- a/solution.py
+++ b/solution.py
@@ -245,8 +245,23 @@
     return lands + [pltpu.SemaphoreType.DMA((8,))] * 2
 
 
-def convolve(pad, taps, begin, first, last, flip, store):
-    cols, channels = pad.shape[1] - 16, pad.shape[2]
+def shift_columns(pad, shifted):
+    cols = shifted.shape[2]
+
+    def row_step(r, carry):
+        for j in range(7):
+            shifted[j, r] = pad[r, 5 + j : 5 + j + cols]
+        return carry
+
+    lax.fori_loop(0, pad.shape[0], row_step, 0)
+
+
+def shifted_scratch(rows, cols, channels):
+    return pltpu.VMEM((7, rows + 6, cols, channels), jnp.float32)
+
+
+def convolve(shifted, taps, begin, first, last, flip, store):
+    channels = shifted.shape[3]
 
     def row_step(p, carry):
         for h in range(channels // 128):
@@ -256,14 +271,14 @@
                 for j in range(7):
                     t = i * 7 + j
                     t = 48 - t if flip else t
-                    total = total + pad[p + i, 5 + j : 5 + j + cols, lanes] * taps[t : t + 1, lanes]
+                    total = total + shifted[j, p + i, :, lanes] * taps[t : t + 1, lanes]
             store(p, lanes, total)
         return carry
 
     lax.fori_loop(first, last, row_step, 0)
 
 
-def correlate(pad, grad, out):
+def correlate(shifted, grad, out):
     rows, cols, channels = grad.shape
     for h in range(channels // 128):
         lanes = slice(h * 128, (h + 1) * 128)
@@ -273,7 +288,7 @@
                 own = grad[p, :, lanes].astype(jnp.float32)
                 new = []
                 for i in range(7):
-                    term = pad[p + i, 5 + j : 5 + j + cols, lanes] * own
+                    term = shifted[j, p + i, :, lanes] * own
                     new.append(sums[i] + jnp.sum(term.reshape(cols // 8, 8, 128), axis=0))
                 return tuple(new)
 
@@ -284,11 +299,12 @@
                 out[i * 7 + j : i * 7 + j + 1, lanes] = jnp.sum(sums[i], axis=0, keepdims=True)
 
 
-def depth_kernel(state, taps, bias, depth_out, pad, *scratch):
+def depth_kernel(state, taps, bias, depth_out, pad, shifted, *scratch):
     halo = Halo(state, scratch[:8], *scratch[8:])
     greet_neighbours(0)
     halo.start()
     halo.finish(pad)
+    shift_columns(pad, shifted)
     cols = state.shape[1]
 
     def begin(p, lanes):
@@ -297,7 +313,7 @@
     def store(p, lanes, total):
         depth_out[p, :, lanes] = total
 
-    convolve(pad, taps, begin, 0, state.shape[0], False, store)
+    convolve(shifted, taps, begin, 0, state.shape[0], False, store)
 
 
 def depth_of(state, taps, bias):
@@ -311,7 +327,7 @@
         ),
         in_specs=[vmem] * 3,
         out_specs=(vmem,) * 2,
-        scratch_shapes=halo_scratch(rows, cols, channels),
+        scratch_shapes=[shifted_scratch(rows, cols, channels), *halo_scratch(rows, cols, channels)],
         compiler_params=pltpu.CompilerParams(
             collective_id=1, has_side_effects=True, vmem_limit_bytes=40 * 1024 * 1024
         ),
@@ -321,8 +337,8 @@
 def final_kernel(phases, steps, small_steps, wide_ref, tall_ref, other_ref, grad_ref, pad_ref, cot_ref,
                  taps_ref, wide_out, tall_out, small_out, state_out, *scratch):
     num = len(phases)
-    small_mine, mine, whole, small_whole, grad_pad = scratch[:5]
-    scratch = scratch[5:]
+    small_mine, mine, whole, small_whole, grad_pad, shifted = scratch[:6]
+    scratch = scratch[6:]
     halo = Halo(grad_ref, scratch[:8], *scratch[8:10])
     landing = scratch[10 : 10 + num]
     small_landing = scratch[10 + num : 10 + 2 * num]
@@ -345,7 +361,8 @@
         small_mine[49:used] = other_ref[...]
         if used < small_mine.shape[0]:
             small_mine[used:] = jnp.zeros((small_mine.shape[0] - used, channels), jnp.float32)
-        correlate(pad_ref, grad_ref, small_mine)
+        shift_columns(pad_ref, shifted)
+        correlate(shifted, grad_ref, small_mine)
 
     def begin(p, lanes):
         return cot_ref[p, :, lanes].astype(jnp.float32)
@@ -355,10 +372,11 @@
 
     def near_rows():
         halo.finish(grad_pad)
-        convolve(grad_pad, taps_ref, begin, 0, rows // 2, True, store)
+        shift_columns(grad_pad, shifted)
+        convolve(shifted, taps_ref, begin, 0, rows // 2, True, store)
 
     def far_rows():
-        convolve(grad_pad, taps_ref, begin, rows // 2, rows, True, store)
+        convolve(shifted, taps_ref, begin, rows // 2, rows, True, store)
 
     def chain(reducer):
         moves = []
@@ -433,6 +451,7 @@
             pltpu.VMEM((rows, channels), jnp.bfloat16),
             pltpu.VMEM(small, jnp.float32),
             pltpu.VMEM(pad.shape, jnp.float32),
+            shifted_scratch(*grad.shape),
             *halo_scratch(*grad.shape),
             *landings(steps, jnp.bfloat16),
             *landings(small_steps, jnp.float32),

time: 76.3 us -> 75.4 us (0.988)
  Pallas kernels: 52.5 us -> 51.6 us
    pallas_call x1, Pallas kernels: 13.5 us -> 12.6 us  [depth_of(): pl.pallas_call(depth_kernel, out_shape=(jax.ShapeDtypeStruct(state.shape,...]
where the time goes in v3:
time: 75.4 us; the launch traced here: 75 us
  Pallas kernels  51.6 us (68%)
  matrix products  8.24 us (11%)
  local copies, waits for them, and re-layouts  7.82 us (10%)
  other arithmetic  6.47 us (9%)
  between operations  0.88 us (1%)
    pallas_call x1, Pallas kernels, final_of(): pl.pallas_call(functools.partial(final_kernel, phases, steps, small_steps...  39 us
    pallas_call x1, Pallas kernels, depth_of(): pl.pallas_call(depth_kernel, out_shape=(jax.ShapeDtypeStruct(state.shape,...  12.6 us
    unnamed x34, local copies, waits for them, and re-layouts  5.5 us
    dot_general x1, matrix products, backward_tokens(): lax.dot_general(grad_branch, w_out, (((1,), (1,)), ((), ())), preferred_e...  2.17 us
    mul x1, other arithmetic, local(): grad_w_in * factor  2.17 us
    dot_general x1, matrix products, forward_tokens(): jnp.dot(activated, w_out, preferred_element_type=jnp.float32) + b_out  1.73 us
    dot_general x1, matrix products, backward_tokens(): lax.dot_general(grad_pre, w_in, (((1,), (1,)), ((), ())), preferred_eleme...  1.66 us
    dot_general x1, matrix products, weight_terms(): lax.dot_general(normed, grad_pre, dims, preferred_element_type=jnp.float32)  1.59 us

profile of v3, /device:TPU:0, one launch (start us, length us, event | category | flops | bytes accessed | tf_op | source)
XLA Modules:
  0.0 75.0 jit_solution(7131744846777753364)
XLA Ops:
  0.6 0.0 copy-start
  0.7 0.0 copy-start.10
  0.7 0.7 convert_element_type.56
  1.4 0.8 %reshape.118.taps.taps_ref = f32[49,256]{1,0:T(8,128)S(1)} reshape(f32[7,7,256]{2,1,0:T(8,128)} %param.15) | data formatting | bytes 100352 | tf_op jit(solution)/shard_map/reshape | solution.py:530
  2.2 0.0 copy-start.2
  2.3 0.9 %copy-done.2 = bf16[1,6,64,256]{3,2,1,0:T(8,128)(2,1)S(1)} copy-done((bf16[1,6,64,256]{3,2,1,0:T(8,128)(2,1)S(1)}, bf16[1,6,64,256]{3,2,1,0:T(8,128)(2,1)}, u32[]{:S(2)}) %copy-start.2) | copy-done | bytes 196632
  3.2 0.0 copy-start.9
  3.2 0.7 copy-done.9
  3.9 12.6 %shard_map.203 = (f32[6,64,256]{2,1,0:T(8,128)S(1)}, f32[12,80,256]{2,1,0:T(8,128)S(1)}) custom-call(bf16[6,64,256]{2,1,0:T(8,128)(2,1)S(1)} %bitcast.54, f32[49,256]{1,0:T(8,128)S(1)} %reshape.118.taps.taps_ref, f32[1,256]{1,0:T(1,128)S(1)} %bitcast.56), custom_call_target="tpu_custom_call" | custom-call | tf_op jit(solution)/shard_map/pallas_call | solution.py:322
  16.4 0.1 reduce_sum.90
  16.6 0.1 div.15
  16.7 0.0 copy-start.14
  16.7 0.2 multiply_reduce_fusion.2
  16.9 0.1 rsqrt.12
  17.0 0.9 %add_convert_fusion.1 = bf16[384,256]{1,0:T(8,128)(2,1)S(1)} fusion(f32[6,64,256]{2,1,0:T(8,128)S(1)} %get-tuple-element.17, f32[256]{0:T(256)} %param.18, f32[256]{0:T(256)} %param.17, f32[384]{0:T(512)S(1)} %rsqrt.12, f32[384]{0:T(512)S(1)} %div.15), kind=kLoop, calls=%fused_computation.31 | loop fusion | flops 491520 | bytes 594944 | tf_op jit(solution)/shard_map/convert_element_type | solution.py:470
  17.9 0.0 copy-done
  17.9 0.0 copy-done.10
  17.9 0.4 convolution_add_fusion
  18.3 0.0 copy-done.14
  18.3 0.0 copy-start.1
  18.3 0.0 copy-start.3
  18.3 0.0 copy-start.12
  18.3 1.7 %convolution_add_fusion.1 = f32[384,256]{1,0:T(8,128)S(1)} fusion(bf16[1024,256]{1,0:T(8,128)(2,1)} %param.21, f32[256]{0:T(256)S(1)} %copy-done.14, f32[384,1024]{1,0:T(8,128)S(1)} %convolution_add_fusion), kind=kOutput, calls=%fused_computation.14 | convolution fusion | flops 204963840 | bytes 2491392 | tf_op jit(solution)/shard_map/dot_general | solution.py:473
  20.1 0.0 copy-done.1
  20.1 0.0 copy-done.3
  20.1 0.0 copy-done.12
  20.1 0.9 %convert_reduce_fusion.1 = (f32[256]{0:T(256)S(1)}, f32[1,6,64,256]{3,2,1,0:T(8,128)S(1)}, bf16[1,6,64,256]{3,2,1,0:T(8,128)(2,1)}) fusion(f32[256]{0:T(256)S(1)} %copy-done.12, bf16[1,6,64,256]{3,2,1,0:T(8,128)(2,1)S(1)} %copy-done.1, f32[6,64]{1,0:T(8,128)S(1)} %bitcast.58, f32[1,6,64,256]{3,2,1,0:T(8,128)S(1)} %bitcast.57, ...), kind=kLoop, calls=%fused_computation.23 | loop fusion | flops 1081088 | bytes 1379840 | tf_op jit(solution)/shard_map/reduce_sum | solution.py:507
  21.0 0.1 fusion.8
  21.0 0.0 copy-start.13
  21.0 0.7 convolution_convert_fusion.tall_ref
  21.8 0.3 copy-done.13
  22.1 0.0 copy-start.11
  22.1 2.2 %convert_reduce_fusion = (f32[1024]{0:T(1024)S(1)}, bf16[384,1024]{1,0:T(8,128)(2,1)}) fusion(f32[384,1024]{1,0:T(8,128)S(1)} %convolution_add_fusion, bf16[384,256]{1,0:T(8,128)(2,1)S(1)} %get-tuple-element.30, bf16[1024,256]{1,0:T(8,128)(2,1)S(1)} %copy-done.13), kind=kOutput, calls=%fused_computation.9 | convolution fusion | flops 209976320 | bytes 3084288 | tf_op jit(solution)/shard_map/dot_general | solution.py:479
  24.3 1.6 %convolution_convert_fusion.1.wide_ref = bf16[256,1024]{1,0:T(8,128)(2,1)S(1)} fusion(bf16[384,256]{1,0:T(8,128)(2,1)S(1)} %add_convert_fusion.1, bf16[384,1024]{1,0:T(8,128)(2,1)} %get-tuple-element.41), kind=kOutput, calls=%fused_computation.13 | convolution fusion | flops 201588736 | bytes 1507328 | tf_op jit(solution)/shard_map/dot_general | solution.py:501
  25.9 0.0 copy-done.11
  25.9 1.7 %multiply_reduce_fusion = (f32[256]{0:T(256)S(1)}, f32[384]{0:T(512)S(1)}, f32[384]{0:T(512)S(1)}, f32[256]{0:T(256)S(1)}, f32[384,256]{1,0:T(8,128)S(1)}) fusion(f32[6,64,256]{2,1,0:T(8,128)S(1)} %get-tuple-element.17, f32[384]{0:T(512)S(1)} %rsqrt.12, f32[384]{0:T(512)S(1)} %div.15, f32[256]{0:T(256)S(1)} %copy-done.11, ...), kind=kOutput, calls=%fused_computation.25 | convolution fusion | flops 202210048 | bytes 2106368 | tf_op jit(solution)/shard_map/dot_general | solution.py:484
  27.5 0.3 convert_reduce_fusion.2
  27.8 0.1 concatenate.3.other_ref
  28.0 39.0 %shard_map.204 = (bf16[256,1024]{1,0:T(8,128)(2,1)S(1)}, bf16[1024,256]{1,0:T(8,128)(2,1)S(1)}, f32[64,256]{1,0:T(8,128)S(1)}, bf16[6,64,256]{2,1,0:T(8,128)(2,1)S(1)}) custom-call(bf16[256,1024]{1,0:T(8,128)(2,1)S(1)} %convolution_convert_fusion.1.wide_ref, bf16[1024,256]{1,0:T(8,128)(2,1)S(1)} %convolution_convert_fusion.tall_ref, ...), custom_call_target="tpu_custom_call" | custom-call | tf_op jit(solution)/shard_map/pallas_call | solution.py:438
  67.0 0.0 copy-start.4
  67.0 0.8 %copy-done.4 = bf16[1024,256]{1,0:T(8,128)(2,1)} copy-done((bf16[1024,256]{1,0:T(8,128)(2,1)}, bf16[1024,256]{1,0:T(8,128)(2,1)S(1)}, u32[]{:S(2)}) %copy-start.4) | copy-done | bytes 524312
  67.8 0.0 copy-start.6
  67.8 0.8 %copy-done.6 = bf16[256,1024]{1,0:T(8,128)(2,1)} copy-done((bf16[256,1024]{1,0:T(8,128)(2,1)}, bf16[256,1024]{1,0:T(8,128)(2,1)S(1)}, u32[]{:S(2)}) %copy-start.6) | copy-done | bytes 524312
  68.6 0.0 copy-start.7
  68.6 0.7 copy-done.7
  69.3 0.0 copy-start.5
  69.3 0.6 copy.24
  69.9 0.6 fusion.10
  70.5 0.6 reshape.123
  71.1 0.0 copy-start.8
  71.1 2.2 %convert_multiply_fusion.1 = f32[256,1024]{1,0:T(8,128)} fusion(bf16[256,1024]{1,0:T(8,128)(2,1)} %copy-done.6), kind=kLoop, calls=%fused_computation.16 | loop fusion | flops 524288 | bytes 1572864 | tf_op jit(solution)/shard_map/mul | solution.py:580
  73.3 0.0 copy-done.5
  73.3 1.1 %convert_multiply_fusion = f32[1024,256]{1,0:T(8,128)} fusion(bf16[1024,256]{1,0:T(8,128)(2,1)S(1)} %copy-done.5), kind=kLoop, calls=%fused_computation.15 | loop fusion | flops 524288 | bytes 1572864 | tf_op jit(solution)/shard_map/mul | solution.py:582
  74.4 0.0 copy-done.8
  74.4 0.7 copy.28
  (8 shorter events, 0.0 us)
Async XLA Ops:
  0.6 17.2 %copy-start = (bf16[256,1024]{1,0:T(8,128)(2,1)S(1)}, bf16[256,1024]{1,0:T(8,128)(2,1)}, u32[]{:S(2)}) copy-start(bf16[256,1024]{1,0:T(8,128)(2,1)} %param.19) | copy-start | bytes 1572868
  0.7 17.2 %copy-start.10 = (f32[1024]{0:T(1024)S(1)}, f32[1024]{0:T(1024)}, u32[]{:S(2)}) copy-start(f32[1024]{0:T(1024)} %param.20) | copy-start | bytes 12292
  2.2 0.9 %copy-start.2 = (bf16[1,6,64,256]{3,2,1,0:T(8,128)(2,1)S(1)}, bf16[1,6,64,256]{3,2,1,0:T(8,128)(2,1)}, u32[]{:S(2)}) copy-start(bf16[1,6,64,256]{3,2,1,0:T(8,128)(2,1)} %param.12) | copy-start | bytes 589828
  3.2 0.7 copy-start.9
  16.7 1.6 %copy-start.14 = (f32[256]{0:T(256)S(1)}, f32[256]{0:T(256)}, u32[]{:S(2)}) copy-start(f32[256]{0:T(256)} %param.22) | copy-start | bytes 3076
  18.3 1.8 %copy-start.1 = (bf16[1,6,64,256]{3,2,1,0:T(8,128)(2,1)S(1)}, bf16[1,6,64,256]{3,2,1,0:T(8,128)(2,1)}, u32[]{:S(2)}) copy-start(bf16[1,6,64,256]{3,2,1,0:T(8,128)(2,1)} %param.14) | copy-start | bytes 589828
  18.3 1.8 %copy-start.3 = (bf16[1,6,64,256]{3,2,1,0:T(8,128)(2,1)S(1)}, bf16[1,6,64,256]{3,2,1,0:T(8,128)(2,1)}, u32[]{:S(2)}) copy-start(bf16[1,6,64,256]{3,2,1,0:T(8,128)(2,1)} %param.12) | copy-start | bytes 589828
  18.3 1.8 %copy-start.12 = (f32[256]{0:T(256)S(1)}, f32[256]{0:T(256)}, u32[]{:S(2)}) copy-start(f32[256]{0:T(256)} %param.23) | copy-start | bytes 3076
  21.0 1.0 %copy-start.13 = (bf16[1024,256]{1,0:T(8,128)(2,1)S(1)}, bf16[1024,256]{1,0:T(8,128)(2,1)}, u32[]{:S(2)}) copy-start(bf16[1024,256]{1,0:T(8,128)(2,1)} %param.21) | copy-start | bytes 1572868
  22.1 3.8 %copy-start.11 = (f32[256]{0:T(256)S(1)}, f32[256]{0:T(256)}, u32[]{:S(2)}) copy-start(f32[256]{0:T(256)} %param.17) | copy-start | bytes 3076
  67.0 0.8 %copy-start.4 = (bf16[1024,256]{1,0:T(8,128)(2,1)}, bf16[1024,256]{1,0:T(8,128)(2,1)S(1)}, u32[]{:S(2)}) copy-start(bf16[1024,256]{1,0:T(8,128)(2,1)S(1)} %get-tuple-element.22) | copy-start | bytes 1572868
  67.8 0.8 %copy-start.6 = (bf16[256,1024]{1,0:T(8,128)(2,1)}, bf16[256,1024]{1,0:T(8,128)(2,1)S(1)}, u32[]{:S(2)}) copy-start(bf16[256,1024]{1,0:T(8,128)(2,1)S(1)} %get-tuple-element.21) | copy-start | bytes 1572868
  68.6 0.7 copy-start.7
  69.3 4.0 %copy-start.5 = (bf16[1024,256]{1,0:T(8,128)(2,1)S(1)}, bf16[1024,256]{1,0:T(8,128)(2,1)}, u32[]{:S(2)}) copy-start(bf16[1024,256]{1,0:T(8,128)(2,1)} %copy-done.4) | copy-start | bytes 1572868
  71.1 3.2 %copy-start.8 = (bf16[6,64,256]{2,1,0:T(8,128)(2,1)S(1)}, bf16[6,64,256]{2,1,0:T(8,128)(2,1)}, u32[]{:S(2)}) copy-start(bf16[6,64,256]{2,1,0:T(8,128)(2,1)} %copy-done.7) | copy-start | bytes 589828
